TPU v7x, 128 devices: a whole 4x4x4 slice. The times are simulated.
128 devices in a mesh: tm: 32 (over y, z, core), feat: 4 (over x).
Axes of the slice: x: 4, y: 4, z: 4, core: 2. Of those that a mesh axis runs over, the one named last changes fastest.
Arguments:
- snapshots: bfloat16 [8192, 512], P('tm'), may hold values from -6 to 6
- projection: bfloat16 [4096, 8192], P(None, 'feat'), may hold values from -0.09375 to 0.09375
- phase_shift: float32 [8192], P('feat'), may hold values from -3.140625 to 3.140625
Outputs:
- gram: float32 [8192, 2048], P('feat', 'tm')
- cross: float32 [8192, 2048], P('feat', 'tm')
All inputs are finite; a program needn't handle non-finite values.
Results may differ from a plain program's by a relative error of at most 0.0003.
Values may be sent and summed in bfloat16 or wider, within the bound.
No kernel may reach another device: no remote copies, remote signals or barrier semaphores. Data moves between devices by JAX's collectives and lax.ppermute only.
A program may use at most 128 MiB of HBM per device.

v0:
```python
import functools
import math

import jax
import jax.numpy as jnp
import numpy as np
from jax import lax
from jax.experimental import pallas as pl
from jax.experimental.pallas import tpu as pltpu
from jax.sharding import PartitionSpec as P

CWD = 512
Y, Z, C = 4, 4, 2
LAGS = 8
BLOCK = 256
VMEM, ALMOST_ALL = 20 << 20, 42 << 20

ROUNDER = 1.5 * 2**23


def half_cos_terms():
    fit = np.polynomial.chebyshev.Chebyshev.interpolate(
        lambda q: np.cos(np.sqrt(q) * math.pi), 4, domain=[0.0, (0.5 * 1.0005) ** 2]
    )
    return [float(v * math.sqrt(2 * math.sqrt(2.0))) for v in fit.convert(kind=np.polynomial.Polynomial).coef]


TERMS = half_cos_terms()


def feature(projected, shift):
    turns = (projected + shift) * (1 / (2 * math.pi))
    rest = turns - ((turns + ROUNDER) - ROUNDER)
    q = rest * rest
    p = TERMS[4]
    for term in TERMS[3::-1]:
        p = p * q + term
    return p * p - math.sqrt(2.0)


def split(value):
    high = value.astype(jnp.bfloat16)
    return high, (value - high.astype(jnp.float32)).astype(jnp.bfloat16)


SCALE, POWER = 32.0, 15.5


def encode(value):
    size = jnp.abs(value) * (1 / SCALE)
    level = jnp.log2(size + jnp.sqrt(size * size + 1.0)) * POWER
    return jnp.exp2(jnp.where(value < 0, -level, level)).astype(jnp.bfloat16)


def decode(code):
    root = jnp.exp2(jnp.log2(code.astype(jnp.float32)) * (1 / POWER))
    return (root - 1.0 / root) * (SCALE / 2)


def move(value, to):
    pairs = []
    for y in range(Y):
        for z in range(Z):
            for c in range(C):
                goal = to(y, z, c)
                if goal is not None:
                    gy, gz, gc = goal
                    pairs.append(((y * Z + z) * C + c, (gy % Y * Z + gz % Z) * C + gc % C))
    return lax.ppermute(value, "tm", pairs)


def swap(value):
    return move(value, lambda y, z, c: (y, z, 1 - c))


def around(value, by):
    return lax.ppermute(value, "feat", [(i, (i + by) % 4) for i in range(4)])


def lag_kernel(place, own_ref, *refs):
    others_ref, edge_ref, lagged = refs[4:]
    z, c = place[1], place[2]
    few = own_ref.shape[1]
    rows = few * Z * C
    mine = [own_ref, *refs[:3]]
    theirs = [refs[3], others_ref.at[0], others_ref.at[1], others_ref.at[2]]
    for core, held in ((c, mine), (1 - c, theirs)):
        for r, ref in enumerate(held):
            start = pl.multiple_of((lax.rem(z - r + Z, Z) * C + core) * few, few)
            lagged[7:15, pl.ds(start, few), :] = ref[...]
    at = lax.broadcasted_iota(jnp.int32, (rows, own_ref.shape[2]), 0)
    for i in range(1, LAGS):
        older = pltpu.roll(lagged[7 + i].astype(jnp.float32), 1, 0)
        edge = edge_ref[0, i : i + 1].astype(jnp.float32)
        lagged[i - 1] = jnp.where(at == 0, edge, older).astype(jnp.bfloat16)
    newer = pltpu.roll(lagged[7].astype(jnp.float32), rows - 1, 0)
    edge = edge_ref[1, 0:1].astype(jnp.float32)
    lagged[15] = jnp.where(at == rows - 1, edge, newer).astype(jnp.bfloat16)


def lag(place, own, other, others, edge):
    few, pcs = other.shape[1:]
    return pl.pallas_call(
        lag_kernel,
        out_shape=jax.ShapeDtypeStruct((16, few * Z * C, pcs), jnp.bfloat16),
        in_specs=[pl.BlockSpec(memory_space=pltpu.SMEM)] + [pl.BlockSpec(memory_space=pltpu.VMEM)] * 7,
        out_specs=pl.BlockSpec(memory_space=pltpu.VMEM),
        compiler_params=pltpu.CompilerParams(vmem_limit_bytes=VMEM),
        cost_estimate=pl.CostEstimate(flops=1 << 20, bytes_accessed=1 << 20, transcendentals=0),
        name="lag",
    )(place, *own, other, others, edge)


def prepare_kernel(place, p_ref, shift_ref, piece_ref, mine_ref, sems):
    z, c = place[1], place[2]
    depth, width = mine_ref.shape
    half = depth // C
    columns = pl.ds(pl.multiple_of(z * width, width), width)
    rows = pl.ds(pl.multiple_of(c * half, half), half)
    whole = pltpu.make_async_copy(p_ref.at[:, columns], mine_ref, sems.at[0])
    part = pltpu.make_async_copy(p_ref.at[rows, columns], piece_ref.at[pl.ds(0, half), :], sems.at[1])
    part.start()
    whole.start()
    rest = shift_ref[:, columns]
    at = lax.broadcasted_iota(jnp.int32, (16, width), 0)
    terms = jnp.zeros((16, width), jnp.float32)
    for i in range(3):
        term = rest.astype(jnp.bfloat16).astype(jnp.float32)
        terms = jnp.where(at == i, term, terms)
        rest = rest - term
    piece_ref[half : half + 16, :] = terms.astype(jnp.bfloat16)
    part.wait()
    whole.wait()


def prepare(place, projection, shift):
    depth, width = projection.shape[0], CWD // Z
    return pl.pallas_call(
        prepare_kernel,
        out_shape=[
            jax.ShapeDtypeStruct((depth // C + 16, width), jnp.bfloat16),
            jax.ShapeDtypeStruct((depth, width), jnp.bfloat16),
        ],
        in_specs=[
            pl.BlockSpec(memory_space=pltpu.SMEM),
            pl.BlockSpec(memory_space=pltpu.HBM),
            pl.BlockSpec(memory_space=pltpu.VMEM),
        ],
        out_specs=[pl.BlockSpec(memory_space=pltpu.VMEM)] * 2,
        scratch_shapes=[pltpu.SemaphoreType.DMA((2,))],
        compiler_params=pltpu.CompilerParams(vmem_limit_bytes=ALMOST_ALL),
        cost_estimate=pl.CostEstimate(flops=0, bytes_accessed=3 << 20, transcendentals=0),
        name="prepare",
    )(place, projection, shift)


def share_kernel(place, p_ref, share_ref, sem):
    width = share_ref.shape[1]
    copy = pltpu.make_async_copy(p_ref.at[:, pl.ds(pl.multiple_of(place[2] * width, width), width)], share_ref, sem)
    copy.start()
    copy.wait()


def share_of(place, projection):
    depth, width = projection.shape
    return pl.pallas_call(
        share_kernel,
        out_shape=jax.ShapeDtypeStruct((depth, width // C), jnp.bfloat16),
        in_specs=[pl.BlockSpec(memory_space=pltpu.SMEM), pl.BlockSpec(memory_space=pltpu.HBM)],
        out_specs=pl.BlockSpec(memory_space=pltpu.VMEM),
        scratch_shapes=[pltpu.SemaphoreType.DMA],
        compiler_params=pltpu.CompilerParams(vmem_limit_bytes=ALMOST_ALL),
        cost_estimate=pl.CostEstimate(flops=0, bytes_accessed=8 << 20, transcendentals=0),
        name="share",
    )(place, projection)


def feats_kernel(first, place, lagged, p_ref, shift_ref, high_ref, low_ref):
    rows = lagged.shape[1]
    half = p_ref.shape[1]
    pairs = LAGS // 2
    for n in range(high_ref.shape[1] // BLOCK):
        column = (first + n) * BLOCK
        right = p_ref[:, column : column + BLOCK]
        shift = shift_ref[:, pl.ds(pl.multiple_of(place[2] * half + column, BLOCK), BLOCK)]

        def put(at, value):
            to = (slice(at * rows, (at + 1) * rows), slice(n * BLOCK, (n + 1) * BLOCK))
            high_ref[to], low_ref[to] = split(value)

        for i in range(LAGS):
            left = jnp.concatenate([lagged[7 + i - k] for k in range(LAGS)], 1)
            value = feature(jnp.dot(left, right, preferred_element_type=jnp.float32), shift)
            put(i // 2 + (i % 2) * 2 * pairs, value)
            if i % 2 == 0:
                even = value
            else:
                put(i // 2 + pairs, even + value)


def feats_of(first, blocks, place, lagged, projection, shift):
    rows = lagged.shape[1]
    depth = projection.shape[0]
    out = jax.ShapeDtypeStruct((LAGS * 3 // 2 * rows, blocks * BLOCK), jnp.bfloat16)
    return pl.pallas_call(
        functools.partial(feats_kernel, first),
        out_shape=(out, out),
        in_specs=[pl.BlockSpec(memory_space=pltpu.SMEM)] + [pl.BlockSpec(memory_space=pltpu.VMEM)] * 3,
        out_specs=[pl.BlockSpec(memory_space=pltpu.VMEM)] * 2,
        compiler_params=pltpu.CompilerParams(vmem_limit_bytes=VMEM),
        cost_estimate=pl.CostEstimate(
            flops=3 * LAGS * rows * depth * blocks * BLOCK, bytes_accessed=2 * depth * blocks * BLOCK, transcendentals=0
        ),
        name="feats",
    )(place, lagged, projection, shift)


def window_kernel(place, *refs):
    lagged, mine_ref = refs[:2]
    near_refs, swapped_refs = refs[2:5], refs[5:8]
    shift_ref, high_ref, low_ref = refs[8:]
    rows = lagged.shape[1]
    y, c, x = place[0], place[2], place[3]
    depth = mine_ref.shape[0] // C
    lags = LAGS // C
    sides = []
    for own, others in ((c, near_refs), (1 - c, swapped_refs)):
        mine = mine_ref[pl.ds(pl.multiple_of(own * depth, depth), depth), :]
        sides.append((own * lags, jnp.concatenate([mine] + [ref[:depth] for ref in others], 1)))
    parts = [jnp.sum(ref[depth : depth + 16].astype(jnp.float32), 0, keepdims=True) for ref in near_refs]
    shift = jnp.concatenate([shift_ref[...]] + parts, 1)
    at = lax.broadcasted_iota(jnp.int32, (rows, 1), 0)

    def put(place_at, value):
        high, low = split(value)
        width = CWD // Y
        columns = slice(place_at * rows, (place_at + 1) * rows)
        for slot, r in enumerate((0, 1, 3, 2)):
            by = lax.rem(x - r - y + 2 * Y, Y)
            to, of = pl.ds(pl.multiple_of(by * width, width), width), slice(slot * width, (slot + 1) * width)
            high_ref[to, columns] = high[of]
            low_ref[to, columns] = low[of]

    for i in range(LAGS + 1):
        if i < LAGS:
            projected = 0.0
            for first, right in sides:
                left = jnp.concatenate([lagged[7 + i - k - first] for k in range(lags)], 1)
                if i == LAGS - 1:
                    last = [lagged[8 + i - k - first, rows - 16 : rows, :] for k in range(lags)]
                    left = jnp.concatenate([left, jnp.concatenate(last, 1)], 0)
                projected += jnp.dot(left, right, preferred_element_type=jnp.float32)
            values = feature(projected, shift)
            value = values[:rows]
            if i == 0:
                start = value
        else:
            last = jnp.where(y == Y - 1, 0.0, values[rows + 15 : rows + 16])
            value = jnp.where(at == rows - 1, last, pltpu.roll(start, rows - 1, 0))
        value = value.T
        if i > 0:
            put((i - 1) // 2 + ((i - 1) % 2) * LAGS, previous - value)
        if i % 2 == 1:
            put(i // 2 + LAGS // 2, value)
        previous = value


def window_of(place, lagged, mine, near, swapped, shift):
    rows, pcs = lagged.shape[1:]
    out = jax.ShapeDtypeStruct((CWD, LAGS * 3 // 2 * rows), jnp.bfloat16)
    return pl.pallas_call(
        window_kernel,
        out_shape=(out, out),
        in_specs=[pl.BlockSpec(memory_space=pltpu.SMEM)] + [pl.BlockSpec(memory_space=pltpu.VMEM)] * 9,
        out_specs=[pl.BlockSpec(memory_space=pltpu.VMEM)] * 2,
        compiler_params=pltpu.CompilerParams(vmem_limit_bytes=VMEM),
        cost_estimate=pl.CostEstimate(flops=1 << 33, bytes_accessed=8 << 20, transcendentals=0),
        name="window",
    )(place, lagged, mine, *near, *swapped, shift)


def products_kernel(wh_ref, wl_ref, fh_ref, fl_ref, own_ref, *code_refs):
    third = fh_ref.shape[0] // 3
    width = own_ref.shape[1]
    for n in range(fh_ref.shape[1] // BLOCK):
        columns = slice(n * BLOCK, (n + 1) * BLOCK)
        terms = []
        for part in range(3):
            span = slice(part * third, (part + 1) * third)
            total = jnp.dot(wh_ref[:, span], fh_ref[span, columns], preferred_element_type=jnp.float32)
            total += jnp.dot(wl_ref[:, span], fh_ref[span, columns], preferred_element_type=jnp.float32)
            total += jnp.dot(wh_ref[:, span], fl_ref[span, columns], preferred_element_type=jnp.float32)
            terms.append(total)
        for which, total in enumerate((terms[0] + terms[1], terms[1] - terms[2])):
            own_ref[which, :, columns] = total[:width]
            for by, ref in enumerate(code_refs, 1):
                ref[which, :, columns] = encode(total[by * width : (by + 1) * width])


def products_of(wh, wl, fh, fl):
    width = fh.shape[1]
    part = CWD // Y
    return pl.pallas_call(
        products_kernel,
        out_shape=[jax.ShapeDtypeStruct((2, part, width), jnp.float32)]
        + [jax.ShapeDtypeStruct((2, part, width), jnp.bfloat16)] * 3,
        in_specs=[pl.BlockSpec(memory_space=pltpu.VMEM)] * 4,
        out_specs=[pl.BlockSpec(memory_space=pltpu.VMEM)] * 4,
        compiler_params=pltpu.CompilerParams(vmem_limit_bytes=VMEM),
        cost_estimate=pl.CostEstimate(flops=1 << 20, bytes_accessed=1 << 20, transcendentals=0),
        name="products",
    )(wh, wl, fh, fl)


def after(values, *others):
    return lax.optimization_barrier((values, others))[0]


def local(snapshots, projection, phase_shift):
    rows, pcs = snapshots.shape
    position = lax.axis_index("tm")
    y, z, c = position // (Z * C), position // C % Z, position % C
    x = lax.axis_index("feat")
    place = jnp.stack([y, z, c, x])

    phased = jnp.swapaxes(snapshots.reshape(rows // LAGS, LAGS, pcs), 0, 1)
    ahead, behind, opposite = (move(phased, lambda y, z, c, by=by: (y, z + by, c)) for by in (1, 3, 2))
    own = [phased, ahead, opposite, behind]
    other = swap(phased)
    octets = jnp.stack([jnp.where(c == 1, piece[:, -1], piece[:, 0]) for piece in own])
    octet = lax.dynamic_index_in_dim(octets, jnp.where(c == 1, (z + 1) % Z, z), 0, keepdims=False)

    octet = after(octet, other)
    others = swap(jnp.stack(own[1:]))

    def outward(core):
        def to(y, z, c):
            gy = y + 1 if c == 1 else y - 1
            return (gy, z, c if core == 0 else 1 - c) if 0 <= gy < Y else None

        return move(octet, to)

    straight, crossed = outward(0), outward(1)
    edge = jnp.where(c == 1, jnp.stack([straight, crossed]), jnp.stack([crossed, straight]))

    width = CWD // Z
    phases = phase_shift[None]
    piece, mine = prepare(place, projection, phases)
    share = share_of(after(place, ahead), projection)
    shift = lax.dynamic_slice_in_dim(phase_shift, z * width, width, 0)[None]
    piece = after(piece, other)
    near = [around(piece, by) for by in (1, 3)]
    lagged = lag(place, own, other, after(others, near), edge)
    swapped = [swap(v) for v in after(near, lagged)]
    near = [*near, around(after(piece, lagged), 2)]

    def feats(first, blocks, *others):
        return feats_of(first, blocks, place, after(lagged, *others), share, phases)

    def send(codes):
        return [move(codes[by - 1], lambda y, z, c, by=by: (y + by, z, c)) for by in (1, 3, 2)]

    f0 = feats(0, 2, shift)
    swapped = [*after(swapped, f0), swap(after(near[2], f0))]
    w = window_of(place, lagged, mine, near, swapped, shift)
    own0, *codes0 = products_of(*w, *f0)
    sent0 = send(codes0)
    f1 = feats(2, 2, own0)
    own1, *codes1 = products_of(*w, *after(f1, own0))
    sent0 = after(sent0, own1)
    sent1 = send(after(codes1, sent0))
    part = width // C

    def finish(chunks):
        total = jnp.concatenate([own + sum(decode(v) for v in sent) for own, sent in chunks], 2)
        low, high = total[:, :part], total[:, part:]
        return jnp.where(c == 1, high, low), swap(jnp.where(c == 1, low, high))

    most = finish(after([(own0, sent0)], own1))
    rest = finish([(own1, sent1)])
    ours, theirs = (jnp.concatenate(v, 2) for v in zip(most, rest))
    whole = jnp.where(c == 1, jnp.concatenate([theirs, ours], 2), jnp.concatenate([ours, theirs], 2))
    steps = rows * Y * Z * C
    return whole[0].T / steps, whole[1].T / (steps - 1)


def solution(mesh):
    in_specs = (P("tm", None), P(None, "feat"), P("feat"))
    out_specs = (P("feat", "tm"), P("feat", "tm"))
    return jax.shard_map(local, mesh=mesh, in_specs=in_specs, out_specs=out_specs, check_vma=False)
```

profile of v0, /device:TPU:1, one launch (start us, length us, event | category | flops | bytes accessed | tf_op | source)
XLA Modules:
  0.0 120.5 jit_solution(12158977723295054651)
XLA Ops:
  0.6 1.0 copy.39
  1.7 1.5 %collective-permute-start.3 = (bf16[8,32,512]{2,1,0:T(8,128)(2,1)S(1)}, bf16[8,32,512]{2,1,0:T(8,128)(2,1)S(1)}, u32[]{:S(2)}, u32[]{:S(2)}) collective-permute-start(bf16[8,32,512]{2,1,0:T(8,128)(2,1)S(1)} %bitcast.38), channel_id=1, source_target_pairs={{0,4},{4,0},{8,12},{12,8},{16,20},{20,16},{24,28},{28,24},{32,36},... | collective-permute-start | bytes 786440 | tf_op jit(solution)/shard_map/ppermute | solution.py:69
  3.2 3.9 %collective-permute-start.2 = (bf16[8,32,512]{2,1,0:T(8,128)(2,1)S(1)}, bf16[8,32,512]{2,1,0:T(8,128)(2,1)S(1)}, u32[]{:S(2)}, u32[]{:S(2)}) collective-permute-start(bf16[8,32,512]{2,1,0:T(8,128)(2,1)S(1)} %bitcast.39), channel_id=1, source_target_pairs={{0,24},{4,28},{8,0},{12,4},{16,8},{20,12},{24,16},{28,20},{32,56},... | collective-permute-start | bytes 786440 | tf_op jit(solution)/shard_map/ppermute | solution.py:69
  7.0 0.0 collective-permute-start.1
  7.0 0.7 collective-permute-start
  7.8 0.1 pad_add_fusion.place
  7.8 0.7 copy-done
  8.5 2.0 %prepare.1 = (bf16[2064,128]{1,0:T(8,128)(2,1)S(1)}, bf16[4096,128]{1,0:T(8,128)(2,1)S(1)}) custom-call(s32[4]{0:T(128)S(1)} %pad_add_fusion.place, bf16[4096,2048]{1,0:T(8,128)(2,1)} %p_ref.3, f32[1,2048]{1,0:T(1,128)S(1)} %bitcast.47), custom_call_target="tpu_custom_call" | custom-call | bytes 3145728 | tf_op jit(solution)/shard_map/prepare/pallas_call | solution.py:138
  10.5 2.5 %collective-permute-start.6 = (bf16[2064,128]{1,0:T(8,128)(2,1)S(1)}, bf16[2064,128]{1,0:T(8,128)(2,1)S(1)}, u32[]{:S(2)}, u32[]{:S(2)}) collective-permute-start(bf16[2064,128]{1,0:T(8,128)(2,1)S(1)} %get-tuple-element.47), channel_id=1, source_target_pairs={{0,3},{1,0},{2,1},{3,2},{4,7},{5,4},{6,5},{7,6},{8,11},{9,8},{10,9... | collective-permute-start | bytes 1585160 | tf_op jit(solution)/shard_map/ppermute | solution.py:77
  13.1 5.2 %collective-permute-done.2.refs_2_ = bf16[8,32,512]{2,1,0:T(8,128)(2,1)S(1)} collective-permute-done((bf16[8,32,512]{2,1,0:T(8,128)(2,1)S(1)}, bf16[8,32,512]{2,1,0:T(8,128)(2,1)S(1)}, u32[]{:S(2)}, u32[]{:S(2)}) %collective-permute-start.2) | collective-permute-done | bytes 262176 | tf_op jit(solution)/shard_map/ppermute | solution.py:69
  18.4 3.5 %collective-permute-done.refs_0_ = bf16[8,32,512]{2,1,0:T(8,128)(2,1)S(1)} collective-permute-done((bf16[8,32,512]{2,1,0:T(8,128)(2,1)S(1)}, bf16[8,32,512]{2,1,0:T(8,128)(2,1)S(1)}, u32[]{:S(2)}, u32[]{:S(2)}) %collective-permute-start) | collective-permute-done | bytes 262176 | tf_op jit(solution)/shard_map/ppermute | solution.py:69
  21.8 0.1 pad_maximum_fusion
  21.9 0.8 collective-permute-start.4
  22.9 3.1 %collective-permute-start.8 = (bf16[8,512]{1,0:T(8,128)(2,1)S(1)}, bf16[8,512]{1,0:T(8,128)(2,1)S(1)}, u32[]{:S(2)}, u32[]{:S(2)}) collective-permute-start(bf16[8,512]{1,0:T(8,128)(2,1)S(1)} %fusion.13), channel_id=1, source_target_pairs={{4,32},{12,40},{20,48},{28,56},{32,4},{36,64},{40,12},{44,72},{48,... | collective-permute-start | bytes 24584 | tf_op jit(solution)/shard_map/ppermute | solution.py:69
  26.0 3.2 %collective-permute-start.7 = (bf16[8,512]{1,0:T(8,128)(2,1)S(1)}, bf16[8,512]{1,0:T(8,128)(2,1)S(1)}, u32[]{:S(2)}, u32[]{:S(2)}) collective-permute-start(bf16[8,512]{1,0:T(8,128)(2,1)S(1)} %fusion.13), channel_id=1, source_target_pairs={{4,36},{12,44},{20,52},{28,60},{32,0},{36,68},{40,8},{44,76},{48,1... | collective-permute-start | bytes 24584 | tf_op jit(solution)/shard_map/ppermute | solution.py:69
  29.2 0.1 dynamic-slice_bitcast_fusion.refs_8_
  29.3 3.9 %share.1.p_ref = bf16[4096,1024]{1,0:T(8,128)(2,1)S(1)} custom-call(s32[4]{0:T(128)S(1)} %pad_add_fusion.place, bf16[4096,2048]{1,0:T(8,128)(2,1)} %p_ref.3), custom_call_target="tpu_custom_call" | custom-call | bytes 8388608 | tf_op jit(solution)/shard_map/share/pallas_call | solution.py:166
  33.2 0.0 collective-permute-done.8
  33.3 0.0 collective-permute-done.6.refs_3_
  33.3 0.0 collective-permute-done.5.refs_2_
  33.3 1.4 %lag.1.lagged.refs_0_ = bf16[16,256,512]{2,1,0:T(8,128)(2,1)S(1)} custom-call(s32[4]{0:T(128)S(1)} %pad_add_fusion.place, bf16[8,32,512]{2,1,0:T(8,128)(2,1)S(1)} %bitcast.43, bf16[8,32,512]{2,1,0:T(8,128)(2,1)S(1)} %collective-permute-done.refs_0_, bf16[8,32,512]{2,1,0:T(8,128)(2,1)S(1)} %collective-permute-done.1.refs_1_, ...), custom_call_target="tpu_custom_call" | custom-call | flops 1048576 | bytes 1048576 | tf_op jit(solution)/shard_map/lag/pallas_call | solution.py:103
  34.7 2.8 %collective-permute-start.9 = (bf16[2064,128]{1,0:T(8,128)(2,1)S(1)}, bf16[2064,128]{1,0:T(8,128)(2,1)S(1)}, u32[]{:S(2)}, u32[]{:S(2)}) collective-permute-start(bf16[2064,128]{1,0:T(8,128)(2,1)S(1)} %get-tuple-element.47), channel_id=1, source_target_pairs={{0,2},{1,3},{2,0},{3,1},{4,6},{5,7},{6,4},{7,5},{8,10},{9,11},{10,... | collective-permute-start | bytes 1585160 | tf_op jit(solution)/shard_map/ppermute | solution.py:77
  37.5 0.0 collective-permute-start.10
  37.5 0.7 collective-permute-start.11
  38.2 11.8 %feats.2 = (bf16[3072,512]{1,0:T(8,128)(2,1)S(1)}, bf16[3072,512]{1,0:T(8,128)(2,1)S(1)}) custom-call(s32[4]{0:T(128)S(1)} %pad_add_fusion.place, bf16[16,256,512]{2,1,0:T(8,128)(2,1)S(1)} %lag.1.lagged.refs_0_, bf16[4096,1024]{1,0:T(8,128)(2,1)S(1)} %share.1.p_ref, f32[1,2048]{1,0:T(1,128)S(1)} %bitcast.48), custom_call_target="tpu_custom_call" | custom-call | flops 12884901888 | bytes 4194304 | tf_op jit(solution)/shard_map/feats/pallas_call | solution.py:205
  50.0 0.0 collective-permute-done.9.refs_4_
  50.0 0.4 collective-permute-start.12
  50.4 0.0 collective-permute-done.10.refs_5_
  50.4 1.9 %collective-permute-done.12.refs_7_ = bf16[2064,128]{1,0:T(8,128)(2,1)S(1)} collective-permute-done((bf16[2064,128]{1,0:T(8,128)(2,1)S(1)}, bf16[2064,128]{1,0:T(8,128)(2,1)S(1)}, u32[]{:S(2)}, u32[]{:S(2)}) %collective-permute-start.12) | collective-permute-done | bytes 528416 | tf_op jit(solution)/shard_map/ppermute | solution.py:69
  52.3 11.5 %window.1 = (bf16[512,3072]{1,0:T(8,128)(2,1)S(1)}, bf16[512,3072]{1,0:T(8,128)(2,1)S(1)}) custom-call(s32[4]{0:T(128)S(1)} %pad_add_fusion.place, bf16[16,256,512]{2,1,0:T(8,128)(2,1)S(1)} %lag.1.lagged.refs_0_, bf16[4096,128]{1,0:T(8,128)(2,1)S(1)} %get-tuple-element.46.refs_1_, bf16[2064,128]{1,0:T(8,128)(2,1)S(1)} %collective-permute-done.5.refs_2_, ...), custom_call_target="tpu_custom_call" | custom-call | flops 8589934592 | bytes 8388608 | tf_op jit(solution)/shard_map/window/pallas_call | solution.py:271
  63.9 16.3 %products.2 = (f32[2,128,512]{2,1,0:T(8,128)S(1)}, bf16[2,128,512]{2,1,0:T(8,128)(2,1)S(1)}, bf16[2,128,512]{2,1,0:T(8,128)(2,1)S(1)}, bf16[2,128,512]{2,1,0:T(8,128)(2,1)S(1)}) custom-call(bf16[512,3072]{1,0:T(8,128)(2,1)S(1)} %get-tuple-element.57.wh_ref, bf16[512,3072]{1,0:T(8,128)(2,1)S(1)} %get-tuple-element.58.wl_ref, ...), custom_call_target="tpu_custom_call" | custom-call | flops 1048576 | bytes 1048576 | tf_op jit(solution)/shard_map/products/pallas_call | solution.py:303
  80.2 1.1 collective-permute-start.13
  81.3 1.7 %collective-permute-start.14 = (bf16[2,128,512]{2,1,0:T(8,128)(2,1)S(1)}, bf16[2,128,512]{2,1,0:T(8,128)(2,1)S(1)}, u32[]{:S(2)}, u32[]{:S(2)}) collective-permute-start(bf16[2,128,512]{2,1,0:T(8,128)(2,1)S(1)} %get-tuple-element.61), channel_id=1, source_target_pairs={{0,96},{4,100},{8,104},{12,108},{16,112},{20,116},{24,120},{28,124... | collective-permute-start | bytes 786440 | tf_op jit(solution)/shard_map/ppermute | solution.py:69
  82.9 0.4 collective-permute-start.15
  83.3 11.8 %feats.3 = (bf16[3072,512]{1,0:T(8,128)(2,1)S(1)}, bf16[3072,512]{1,0:T(8,128)(2,1)S(1)}) custom-call(s32[4]{0:T(128)S(1)} %pad_add_fusion.place, bf16[16,256,512]{2,1,0:T(8,128)(2,1)S(1)} %lag.1.lagged.refs_0_, bf16[4096,1024]{1,0:T(8,128)(2,1)S(1)} %share.1.p_ref, f32[1,2048]{1,0:T(1,128)S(1)} %bitcast.49), custom_call_target="tpu_custom_call" | custom-call | flops 12884901888 | bytes 4194304 | tf_op jit(solution)/shard_map/feats/pallas_call | solution.py:205
  95.1 6.1 %products.3 = (f32[2,128,512]{2,1,0:T(8,128)S(1)}, bf16[2,128,512]{2,1,0:T(8,128)(2,1)S(1)}, bf16[2,128,512]{2,1,0:T(8,128)(2,1)S(1)}, bf16[2,128,512]{2,1,0:T(8,128)(2,1)S(1)}) custom-call(bf16[512,3072]{1,0:T(8,128)(2,1)S(1)} %get-tuple-element.57.wh_ref, bf16[512,3072]{1,0:T(8,128)(2,1)S(1)} %get-tuple-element.58.wl_ref, ...), custom_call_target="tpu_custom_call" | custom-call | flops 1048576 | bytes 1048576 | tf_op jit(solution)/shard_map/products/pallas_call | solution.py:303
  101.2 0.5 collective-permute-start.17
  101.8 2.2 %collective-permute-start.18 = (bf16[2,128,512]{2,1,0:T(8,128)(2,1)S(1)}, bf16[2,128,512]{2,1,0:T(8,128)(2,1)S(1)}, u32[]{:S(2)}, u32[]{:S(2)}) collective-permute-start(bf16[2,128,512]{2,1,0:T(8,128)(2,1)S(1)} %get-tuple-element.80), channel_id=1, source_target_pairs={{0,96},{4,100},{8,104},{12,108},{16,112},{20,116},{24,120},{28,124... | collective-permute-start | bytes 786440 | tf_op jit(solution)/shard_map/ppermute | solution.py:69
  104.0 1.4 %collective-permute-start.19 = (bf16[2,128,512]{2,1,0:T(8,128)(2,1)S(1)}, bf16[2,128,512]{2,1,0:T(8,128)(2,1)S(1)}, u32[]{:S(2)}, u32[]{:S(2)}) collective-permute-start(bf16[2,128,512]{2,1,0:T(8,128)(2,1)S(1)} %get-tuple-element.81), channel_id=1, source_target_pairs={{0,64},{4,68},{8,72},{12,76},{16,80},{20,84},{24,88},{28,92},{32,9... | collective-permute-start | bytes 786440 | tf_op jit(solution)/shard_map/ppermute | solution.py:69
  105.4 0.6 fusion.3
  106.0 1.9 %collective-permute-start.16 = (f32[2,64,512]{2,1,0:T(8,128)S(1)}, f32[2,64,512]{2,1,0:T(8,128)S(1)}, u32[]{:S(2)}, u32[]{:S(2)}) collective-permute-start(f32[2,64,512]{2,1,0:T(8,128)S(1)} %get-tuple-element.84), channel_id=1, source_target_pairs={{0,4},{4,0},{8,12},{12,8},{16,20},{20,16},{24,28},{28,24},{32,36},... | collective-permute-start | bytes 786440 | tf_op jit(solution)/shard_map/ppermute | solution.py:69
  108.0 1.1 collective-permute-done.17
  109.1 6.2 %collective-permute-done.19 = bf16[2,128,512]{2,1,0:T(8,128)(2,1)S(1)} collective-permute-done((bf16[2,128,512]{2,1,0:T(8,128)(2,1)S(1)}, bf16[2,128,512]{2,1,0:T(8,128)(2,1)S(1)}, u32[]{:S(2)}, u32[]{:S(2)}) %collective-permute-start.19) | collective-permute-done | bytes 262176 | tf_op jit(solution)/shard_map/ppermute | solution.py:69
  115.3 0.6 fusion.7
  115.9 2.0 %collective-permute-start.20 = (f32[2,64,512]{2,1,0:T(8,128)S(1)}, f32[2,64,512]{2,1,0:T(8,128)S(1)}, u32[]{:S(2)}, u32[]{:S(2)}) collective-permute-start(f32[2,64,512]{2,1,0:T(8,128)S(1)} %get-tuple-element.86), channel_id=1, source_target_pairs={{0,4},{4,0},{8,12},{12,8},{16,20},{20,16},{24,28},{28,24},{32,36},... | collective-permute-start | bytes 786440 | tf_op jit(solution)/shard_map/ppermute | solution.py:69
  117.9 1.2 collective-permute-done.20
  119.1 0.2 maximum_select_fusion
  119.3 1.1 fusion.8
  (26 shorter events, 0.3 us)
Async XLA Ops:
  1.7 8.9 %collective-permute-start.3 = (bf16[8,32,512]{2,1,0:T(8,128)(2,1)S(1)}, bf16[8,32,512]{2,1,0:T(8,128)(2,1)S(1)}, u32[]{:S(2)}, u32[]{:S(2)}) collective-permute-start(bf16[8,32,512]{2,1,0:T(8,128)(2,1)S(1)} %bitcast.38), channel_id=1, source_target_pairs={{0,4},{4,0},{8,12},{12,8},{16,20},{20,16},{24,28},{28,24},{32,36},... | collective-permute-start | bytes 786440 | tf_op jit(solution)/shard_map/ppermute | solution.py:69
  3.2 15.1 %collective-permute-start.2 = (bf16[8,32,512]{2,1,0:T(8,128)(2,1)S(1)}, bf16[8,32,512]{2,1,0:T(8,128)(2,1)S(1)}, u32[]{:S(2)}, u32[]{:S(2)}) collective-permute-start(bf16[8,32,512]{2,1,0:T(8,128)(2,1)S(1)} %bitcast.39), channel_id=1, source_target_pairs={{0,24},{4,28},{8,0},{12,4},{16,8},{20,12},{24,16},{28,20},{32,56},... | collective-permute-start | bytes 786440 | tf_op jit(solution)/shard_map/ppermute | solution.py:69
  7.0 11.3 %collective-permute-start.1 = (bf16[8,32,512]{2,1,0:T(8,128)(2,1)S(1)}, bf16[8,32,512]{2,1,0:T(8,128)(2,1)S(1)}, u32[]{:S(2)}, u32[]{:S(2)}) collective-permute-start(bf16[8,32,512]{2,1,0:T(8,128)(2,1)S(1)} %bitcast.40), channel_id=1, source_target_pairs={{0,16},{4,20},{8,24},{12,28},{16,0},{20,4},{24,8},{28,12},{32,48},... | collective-permute-start | bytes 786440 | tf_op jit(solution)/shard_map/ppermute | solution.py:69
  7.0 14.8 %collective-permute-start = (bf16[8,32,512]{2,1,0:T(8,128)(2,1)S(1)}, bf16[8,32,512]{2,1,0:T(8,128)(2,1)S(1)}, u32[]{:S(2)}, u32[]{:S(2)}) collective-permute-start(bf16[8,32,512]{2,1,0:T(8,128)(2,1)S(1)} %bitcast.41), channel_id=1, source_target_pairs={{0,8},{4,12},{8,16},{12,20},{16,24},{20,28},{24,0},{28,4},{32,40},... | collective-permute-start | bytes 786440 | tf_op jit(solution)/shard_map/ppermute | solution.py:69
  7.8 0.7 copy-start
  8.5 20.7 %copy-start.1 = (f32[2048]{0:T(1024)S(1)}, f32[2048]{0:T(1024)}, u32[]{:S(2)}) copy-start(f32[2048]{0:T(1024)} %param.5) | copy-start | bytes 24580
  10.5 22.8 %collective-permute-start.6 = (bf16[2064,128]{1,0:T(8,128)(2,1)S(1)}, bf16[2064,128]{1,0:T(8,128)(2,1)S(1)}, u32[]{:S(2)}, u32[]{:S(2)}) collective-permute-start(bf16[2064,128]{1,0:T(8,128)(2,1)S(1)} %get-tuple-element.47), channel_id=1, source_target_pairs={{0,3},{1,0},{2,1},{3,2},{4,7},{5,4},{6,5},{7,6},{8,11},{9,8},{10,9... | collective-permute-start | bytes 1585160 | tf_op jit(solution)/shard_map/ppermute | solution.py:77
  13.1 20.2 %collective-permute-start.5 = (bf16[2064,128]{1,0:T(8,128)(2,1)S(1)}, bf16[2064,128]{1,0:T(8,128)(2,1)S(1)}, u32[]{:S(2)}, u32[]{:S(2)}) collective-permute-start(bf16[2064,128]{1,0:T(8,128)(2,1)S(1)} %get-tuple-element.47), channel_id=1, source_target_pairs={{0,1},{1,2},{2,3},{3,0},{4,5},{5,6},{6,7},{7,4},{8,9},{9,10},{10,1... | collective-permute-start | bytes 1585160 | tf_op jit(solution)/shard_map/ppermute | solution.py:77
  21.9 11.4 %collective-permute-start.4 = (bf16[3,8,32,512]{3,2,1,0:T(8,128)(2,1)S(1)}, bf16[3,8,32,512]{3,2,1,0:T(8,128)(2,1)S(1)}, u32[]{:S(2)}, u32[]{:S(2)}) collective-permute-start(bf16[3,8,32,512]{3,2,1,0:T(8,128)(2,1)S(1)} %pad_maximum_fusion), channel_id=1, source_target_pairs={{0,4},{4,0},{8,12},{12,8},{16,20},{20,16},{24,28},{28,24},{32,36},... | collective-permute-start | bytes 2359304 | tf_op jit(solution)/shard_map/ppermute | solution.py:69
  22.9 10.4 %collective-permute-start.8 = (bf16[8,512]{1,0:T(8,128)(2,1)S(1)}, bf16[8,512]{1,0:T(8,128)(2,1)S(1)}, u32[]{:S(2)}, u32[]{:S(2)}) collective-permute-start(bf16[8,512]{1,0:T(8,128)(2,1)S(1)} %fusion.13), channel_id=1, source_target_pairs={{4,32},{12,40},{20,48},{28,56},{32,4},{36,64},{40,12},{44,72},{48,... | collective-permute-start | bytes 24584 | tf_op jit(solution)/shard_map/ppermute | solution.py:69
  26.0 7.3 %collective-permute-start.7 = (bf16[8,512]{1,0:T(8,128)(2,1)S(1)}, bf16[8,512]{1,0:T(8,128)(2,1)S(1)}, u32[]{:S(2)}, u32[]{:S(2)}) collective-permute-start(bf16[8,512]{1,0:T(8,128)(2,1)S(1)} %fusion.13), channel_id=1, source_target_pairs={{4,36},{12,44},{20,52},{28,60},{32,0},{36,68},{40,8},{44,76},{48,1... | collective-permute-start | bytes 24584 | tf_op jit(solution)/shard_map/ppermute | solution.py:69
  34.7 15.3 %collective-permute-start.9 = (bf16[2064,128]{1,0:T(8,128)(2,1)S(1)}, bf16[2064,128]{1,0:T(8,128)(2,1)S(1)}, u32[]{:S(2)}, u32[]{:S(2)}) collective-permute-start(bf16[2064,128]{1,0:T(8,128)(2,1)S(1)} %get-tuple-element.47), channel_id=1, source_target_pairs={{0,2},{1,3},{2,0},{3,1},{4,6},{5,7},{6,4},{7,5},{8,10},{9,11},{10,... | collective-permute-start | bytes 1585160 | tf_op jit(solution)/shard_map/ppermute | solution.py:77
  37.5 12.9 %collective-permute-start.10 = (bf16[2064,128]{1,0:T(8,128)(2,1)S(1)}, bf16[2064,128]{1,0:T(8,128)(2,1)S(1)}, u32[]{:S(2)}, u32[]{:S(2)}) collective-permute-start(bf16[2064,128]{1,0:T(8,128)(2,1)S(1)} %collective-permute-done.5.refs_2_), channel_id=1, source_target_pairs={{0,4},{4,0},{8,12},{12,8},{16,20},{20,16},{24,28},{28,24},{32,36},... | collective-permute-start | bytes 1585160 | tf_op jit(solution)/shard_map/ppermute | solution.py:69
  37.5 12.9 %collective-permute-start.11 = (bf16[2064,128]{1,0:T(8,128)(2,1)S(1)}, bf16[2064,128]{1,0:T(8,128)(2,1)S(1)}, u32[]{:S(2)}, u32[]{:S(2)}) collective-permute-start(bf16[2064,128]{1,0:T(8,128)(2,1)S(1)} %collective-permute-done.6.refs_3_), channel_id=1, source_target_pairs={{0,4},{4,0},{8,12},{12,8},{16,20},{20,16},{24,28},{28,24},{32,36},... | collective-permute-start | bytes 1585160 | tf_op jit(solution)/shard_map/ppermute | solution.py:69
  50.0 2.3 %collective-permute-start.12 = (bf16[2064,128]{1,0:T(8,128)(2,1)S(1)}, bf16[2064,128]{1,0:T(8,128)(2,1)S(1)}, u32[]{:S(2)}, u32[]{:S(2)}) collective-permute-start(bf16[2064,128]{1,0:T(8,128)(2,1)S(1)} %collective-permute-done.9.refs_4_), channel_id=1, source_target_pairs={{0,4},{4,0},{8,12},{12,8},{16,20},{20,16},{24,28},{28,24},{32,36},... | collective-permute-start | bytes 1585160 | tf_op jit(solution)/shard_map/ppermute | solution.py:69
  80.2 21.0 %collective-permute-start.13 = (bf16[2,128,512]{2,1,0:T(8,128)(2,1)S(1)}, bf16[2,128,512]{2,1,0:T(8,128)(2,1)S(1)}, u32[]{:S(2)}, u32[]{:S(2)}) collective-permute-start(bf16[2,128,512]{2,1,0:T(8,128)(2,1)S(1)} %get-tuple-element.60), channel_id=1, source_target_pairs={{0,32},{4,36},{8,40},{12,44},{16,48},{20,52},{24,56},{28,60},{32,6... | collective-permute-start | bytes 786440 | tf_op jit(solution)/shard_map/ppermute | solution.py:69
  81.3 20.0 %collective-permute-start.14 = (bf16[2,128,512]{2,1,0:T(8,128)(2,1)S(1)}, bf16[2,128,512]{2,1,0:T(8,128)(2,1)S(1)}, u32[]{:S(2)}, u32[]{:S(2)}) collective-permute-start(bf16[2,128,512]{2,1,0:T(8,128)(2,1)S(1)} %get-tuple-element.61), channel_id=1, source_target_pairs={{0,96},{4,100},{8,104},{12,108},{16,112},{20,116},{24,120},{28,124... | collective-permute-start | bytes 786440 | tf_op jit(solution)/shard_map/ppermute | solution.py:69
  82.9 18.3 %collective-permute-start.15 = (bf16[2,128,512]{2,1,0:T(8,128)(2,1)S(1)}, bf16[2,128,512]{2,1,0:T(8,128)(2,1)S(1)}, u32[]{:S(2)}, u32[]{:S(2)}) collective-permute-start(bf16[2,128,512]{2,1,0:T(8,128)(2,1)S(1)} %get-tuple-element.62), channel_id=1, source_target_pairs={{0,64},{4,68},{8,72},{12,76},{16,80},{20,84},{24,88},{28,92},{32,9... | collective-permute-start | bytes 786440 | tf_op jit(solution)/shard_map/ppermute | solution.py:69
  101.2 7.9 %collective-permute-start.17 = (bf16[2,128,512]{2,1,0:T(8,128)(2,1)S(1)}, bf16[2,128,512]{2,1,0:T(8,128)(2,1)S(1)}, u32[]{:S(2)}, u32[]{:S(2)}) collective-permute-start(bf16[2,128,512]{2,1,0:T(8,128)(2,1)S(1)} %get-tuple-element.79), channel_id=1, source_target_pairs={{0,32},{4,36},{8,40},{12,44},{16,48},{20,52},{24,56},{28,60},{32,6... | collective-permute-start | bytes 786440 | tf_op jit(solution)/shard_map/ppermute | solution.py:69
  101.8 7.4 %collective-permute-start.18 = (bf16[2,128,512]{2,1,0:T(8,128)(2,1)S(1)}, bf16[2,128,512]{2,1,0:T(8,128)(2,1)S(1)}, u32[]{:S(2)}, u32[]{:S(2)}) collective-permute-start(bf16[2,128,512]{2,1,0:T(8,128)(2,1)S(1)} %get-tuple-element.80), channel_id=1, source_target_pairs={{0,96},{4,100},{8,104},{12,108},{16,112},{20,116},{24,120},{28,124... | collective-permute-start | bytes 786440 | tf_op jit(solution)/shard_map/ppermute | solution.py:69
  104.0 11.3 %collective-permute-start.19 = (bf16[2,128,512]{2,1,0:T(8,128)(2,1)S(1)}, bf16[2,128,512]{2,1,0:T(8,128)(2,1)S(1)}, u32[]{:S(2)}, u32[]{:S(2)}) collective-permute-start(bf16[2,128,512]{2,1,0:T(8,128)(2,1)S(1)} %get-tuple-element.81), channel_id=1, source_target_pairs={{0,64},{4,68},{8,72},{12,76},{16,80},{20,84},{24,88},{28,92},{32,9... | collective-permute-start | bytes 786440 | tf_op jit(solution)/shard_map/ppermute | solution.py:69
  106.0 11.9 %collective-permute-start.16 = (f32[2,64,512]{2,1,0:T(8,128)S(1)}, f32[2,64,512]{2,1,0:T(8,128)S(1)}, u32[]{:S(2)}, u32[]{:S(2)}) collective-permute-start(f32[2,64,512]{2,1,0:T(8,128)S(1)} %get-tuple-element.84), channel_id=1, source_target_pairs={{0,4},{4,0},{8,12},{12,8},{16,20},{20,16},{24,28},{28,24},{32,36},... | collective-permute-start | bytes 786440 | tf_op jit(solution)/shard_map/ppermute | solution.py:69
  115.9 3.2 %collective-permute-start.20 = (f32[2,64,512]{2,1,0:T(8,128)S(1)}, f32[2,64,512]{2,1,0:T(8,128)S(1)}, u32[]{:S(2)}, u32[]{:S(2)}) collective-permute-start(f32[2,64,512]{2,1,0:T(8,128)S(1)} %get-tuple-element.86), channel_id=1, source_target_pairs={{0,4},{4,0},{8,12},{12,8},{16,20},{20,16},{24,28},{28,24},{32,36},... | collective-permute-start | bytes 786440 | tf_op jit(solution)/shard_map/ppermute | solution.py:69
where the time goes:
time: 120 us; the launch traced here: 121 us
  Pallas kernels  64.8 us (54%)
  starting transfers between devices  30.8 us (26%)
  waiting for transfers between devices  19.1 us (16%)
  other arithmetic  2.9 us (2%)
  local copies, waits for them, and re-layouts  1.83 us (2%)
    ppermute x18, starting transfers between devices, move(): return lax.ppermute(value, 'tm', pairs)  25.5 us
    pallas_call x2, Pallas kernels, feats_of(): pl.pallas_call(functools.partial(feats_kernel, first), out_shape=(out, ou...  23.5 us
    pallas_call x2, Pallas kernels, products_of(): pl.pallas_call(products_kernel, out_shape=[jax.ShapeDtypeStruct((2, part,...  22.5 us
    ppermute x18, waiting for transfers between devices, move(): return lax.ppermute(value, 'tm', pairs)  19 us
    pallas_call x1, Pallas kernels, window_of(): pl.pallas_call(window_kernel, out_shape=(out, out), in_specs=[pl.BlockSpe...  11.5 us
    ppermute x3, starting transfers between devices, around(): return lax.ppermute(value, 'feat', [(i, (i + by) % 4) for i in range(4)])  5.37 us
    pallas_call x1, Pallas kernels, share_of(): pl.pallas_call(share_kernel, out_shape=jax.ShapeDtypeStruct((depth, width...  3.93 us
  transfers between devices with their start and end apart: 21, of which 6 were waited for; matrix products, arithmetic and copies ran while one was open for 1% of the time, Pallas kernels for 29%

commit v1 on v0

--- a/solution.py
+++ b/solution.py
@@ -154,18 +154,19 @@
     )(place, projection, shift)
 
 
-def share_kernel(place, p_ref, share_ref, sem):
+def share_kernel(part, place, p_ref, share_ref, sem):
     width = share_ref.shape[1]
-    copy = pltpu.make_async_copy(p_ref.at[:, pl.ds(pl.multiple_of(place[2] * width, width), width)], share_ref, sem)
+    start = pl.multiple_of((place[2] * 2 + part) * width, width)
+    copy = pltpu.make_async_copy(p_ref.at[:, pl.ds(start, width)], share_ref, sem)
     copy.start()
     copy.wait()
 
 
-def share_of(place, projection):
+def share_of(part, place, projection):
     depth, width = projection.shape
     return pl.pallas_call(
-        share_kernel,
-        out_shape=jax.ShapeDtypeStruct((depth, width // C), jnp.bfloat16),
+        functools.partial(share_kernel, part),
+        out_shape=jax.ShapeDtypeStruct((depth, width // C // 2), jnp.bfloat16),
         in_specs=[pl.BlockSpec(memory_space=pltpu.SMEM), pl.BlockSpec(memory_space=pltpu.HBM)],
         out_specs=pl.BlockSpec(memory_space=pltpu.VMEM),
         scratch_shapes=[pltpu.SemaphoreType.DMA],
@@ -177,11 +178,11 @@
 
 def feats_kernel(first, place, lagged, p_ref, shift_ref, high_ref, low_ref):
     rows = lagged.shape[1]
-    half = p_ref.shape[1]
+    half = shift_ref.shape[1] // C
     pairs = LAGS // 2
     for n in range(high_ref.shape[1] // BLOCK):
         column = (first + n) * BLOCK
-        right = p_ref[:, column : column + BLOCK]
+        right = p_ref[:, n * BLOCK : (n + 1) * BLOCK]
         shift = shift_ref[:, pl.ds(pl.multiple_of(place[2] * half + column, BLOCK), BLOCK)]
 
         def put(at, value):
@@ -346,7 +347,7 @@
     width = CWD // Z
     phases = phase_shift[None]
     piece, mine = prepare(place, projection, phases)
-    share = share_of(after(place, ahead), projection)
+    share = share_of(0, after(place, ahead), projection)
     shift = lax.dynamic_slice_in_dim(phase_shift, z * width, width, 0)[None]
     piece = after(piece, other)
     near = [around(piece, by) for by in (1, 3)]
@@ -354,18 +355,19 @@
     swapped = [swap(v) for v in after(near, lagged)]
     near = [*near, around(after(piece, lagged), 2)]
 
-    def feats(first, blocks, *others):
+    def feats(first, blocks, share, *others):
         return feats_of(first, blocks, place, after(lagged, *others), share, phases)
 
     def send(codes):
         return [move(codes[by - 1], lambda y, z, c, by=by: (y + by, z, c)) for by in (1, 3, 2)]
 
-    f0 = feats(0, 2, shift)
+    f0 = feats(0, 2, share, shift)
+    share = share_of(1, after(place, f0), projection)
     swapped = [*after(swapped, f0), swap(after(near[2], f0))]
-    w = window_of(place, lagged, mine, near, swapped, shift)
+    w = window_of(place, lagged, mine, near, after(swapped, share), shift)
     own0, *codes0 = products_of(*w, *f0)
     sent0 = send(codes0)
-    f1 = feats(2, 2, own0)
+    f1 = feats(2, 2, share, own0)
     own1, *codes1 = products_of(*w, *after(f1, own0))
     sent0 = after(sent0, own1)
     sent1 = send(after(codes1, sent0))

time: 120 us -> 119 us (level)
  waiting for transfers between devices: 19.1 us -> 16.9 us
  Pallas kernels: 64.8 us -> 66 us
    ppermute x18, waiting for transfers between devices: 19 us -> 16.9 us  [move(): return lax.ppermute(value, 'tm', pairs)]
    pallas_call x1 -> x2, Pallas kernels: 3.93 us -> 5.48 us  [share_of(): pl.pallas_call(functools.partial(share_kernel, part), out_shape=jax.Shape...]
  transfers between devices with their start and end apart: 21 -> 21, of which waited for: 6 -> 5; matrix products, arithmetic and copies ran while one was open for 1% -> 1% of each run, Pallas kernels for 29% -> 30%
where the time goes in v1:
time: 119 us; the launch traced here: 120 us
  Pallas kernels  66 us (55%)
  starting transfers between devices  31.5 us (26%)
  waiting for transfers between devices  16.9 us (14%)
  other arithmetic  2.9 us (2%)
  local copies, waits for them, and re-layouts  1.84 us (2%)
    ppermute x18, starting transfers between devices, move(): return lax.ppermute(value, 'tm', pairs)  26.1 us
    pallas_call x2, Pallas kernels, feats_of(): pl.pallas_call(functools.partial(feats_kernel, first), out_shape=(out, ou...  22.9 us
    pallas_call x2, Pallas kernels, products_of(): pl.pallas_call(products_kernel, out_shape=[jax.ShapeDtypeStruct((2, part,...  22.7 us
    ppermute x18, waiting for transfers between devices, move(): return lax.ppermute(value, 'tm', pairs)  16.9 us
    pallas_call x1, Pallas kernels, window_of(): pl.pallas_call(window_kernel, out_shape=(out, out), in_specs=[pl.BlockSpe...  11.6 us
    pallas_call x2, Pallas kernels, share_of(): pl.pallas_call(functools.partial(share_kernel, part), out_shape=jax.Shape...  5.48 us
    ppermute x3, starting transfers between devices, around(): return lax.ppermute(value, 'feat', [(i, (i + by) % 4) for i in range(4)])  5.37 us
  transfers between devices with their start and end apart: 21, of which 5 were waited for; matrix products, arithmetic and copies ran while one was open for 1% of the time, Pallas kernels for 30%

profile of v1, /device:TPU:1, one launch (start us, length us, event | category | flops | bytes accessed | tf_op | source)
XLA Modules:
  0.0 120.2 jit_solution(9753366863702120146)
XLA Ops:
  0.6 1.0 copy.39
  1.7 1.5 %collective-permute-start.3 = (bf16[8,32,512]{2,1,0:T(8,128)(2,1)S(1)}, bf16[8,32,512]{2,1,0:T(8,128)(2,1)S(1)}, u32[]{:S(2)}, u32[]{:S(2)}) collective-permute-start(bf16[8,32,512]{2,1,0:T(8,128)(2,1)S(1)} %bitcast.38), channel_id=1, source_target_pairs={{0,4},{4,0},{8,12},{12,8},{16,20},{20,16},{24,28},{28,24},{32,36},... | collective-permute-start | bytes 786440 | tf_op jit(solution)/shard_map/ppermute | solution.py:69
  3.2 3.9 %collective-permute-start.2 = (bf16[8,32,512]{2,1,0:T(8,128)(2,1)S(1)}, bf16[8,32,512]{2,1,0:T(8,128)(2,1)S(1)}, u32[]{:S(2)}, u32[]{:S(2)}) collective-permute-start(bf16[8,32,512]{2,1,0:T(8,128)(2,1)S(1)} %bitcast.39), channel_id=1, source_target_pairs={{0,24},{4,28},{8,0},{12,4},{16,8},{20,12},{24,16},{28,20},{32,56},... | collective-permute-start | bytes 786440 | tf_op jit(solution)/shard_map/ppermute | solution.py:69
  7.0 0.7 collective-permute-start
  7.8 0.1 pad_add_fusion.place
  7.8 0.7 copy-done
  8.5 2.0 %prepare.1 = (bf16[2064,128]{1,0:T(8,128)(2,1)S(1)}, bf16[4096,128]{1,0:T(8,128)(2,1)S(1)}) custom-call(s32[4]{0:T(128)S(1)} %pad_add_fusion.place, bf16[4096,2048]{1,0:T(8,128)(2,1)} %p_ref.5, f32[1,2048]{1,0:T(1,128)S(1)} %bitcast.47), custom_call_target="tpu_custom_call" | custom-call | bytes 3145728 | tf_op jit(solution)/shard_map/prepare/pallas_call | solution.py:138
  10.5 2.5 %collective-permute-start.6 = (bf16[2064,128]{1,0:T(8,128)(2,1)S(1)}, bf16[2064,128]{1,0:T(8,128)(2,1)S(1)}, u32[]{:S(2)}, u32[]{:S(2)}) collective-permute-start(bf16[2064,128]{1,0:T(8,128)(2,1)S(1)} %get-tuple-element.51), channel_id=1, source_target_pairs={{0,3},{1,0},{2,1},{3,2},{4,7},{5,4},{6,5},{7,6},{8,11},{9,8},{10,9... | collective-permute-start | bytes 1585160 | tf_op jit(solution)/shard_map/ppermute | solution.py:77
  13.1 5.2 %collective-permute-done.2.refs_2_ = bf16[8,32,512]{2,1,0:T(8,128)(2,1)S(1)} collective-permute-done((bf16[8,32,512]{2,1,0:T(8,128)(2,1)S(1)}, bf16[8,32,512]{2,1,0:T(8,128)(2,1)S(1)}, u32[]{:S(2)}, u32[]{:S(2)}) %collective-permute-start.2) | collective-permute-done | bytes 262176 | tf_op jit(solution)/shard_map/ppermute | solution.py:69
  18.3 0.0 collective-permute-done.1.refs_1_
  18.4 3.5 %collective-permute-done.refs_0_ = bf16[8,32,512]{2,1,0:T(8,128)(2,1)S(1)} collective-permute-done((bf16[8,32,512]{2,1,0:T(8,128)(2,1)S(1)}, bf16[8,32,512]{2,1,0:T(8,128)(2,1)S(1)}, u32[]{:S(2)}, u32[]{:S(2)}) %collective-permute-start) | collective-permute-done | bytes 262176 | tf_op jit(solution)/shard_map/ppermute | solution.py:69
  21.8 0.1 pad_maximum_fusion
  21.9 0.8 collective-permute-start.4
  22.9 3.1 %collective-permute-start.8 = (bf16[8,512]{1,0:T(8,128)(2,1)S(1)}, bf16[8,512]{1,0:T(8,128)(2,1)S(1)}, u32[]{:S(2)}, u32[]{:S(2)}) collective-permute-start(bf16[8,512]{1,0:T(8,128)(2,1)S(1)} %fusion.13), channel_id=1, source_target_pairs={{4,32},{12,40},{20,48},{28,56},{32,4},{36,64},{40,12},{44,72},{48,... | collective-permute-start | bytes 24584 | tf_op jit(solution)/shard_map/ppermute | solution.py:69
  26.0 3.2 %collective-permute-start.7 = (bf16[8,512]{1,0:T(8,128)(2,1)S(1)}, bf16[8,512]{1,0:T(8,128)(2,1)S(1)}, u32[]{:S(2)}, u32[]{:S(2)}) collective-permute-start(bf16[8,512]{1,0:T(8,128)(2,1)S(1)} %fusion.13), channel_id=1, source_target_pairs={{4,36},{12,44},{20,52},{28,60},{32,0},{36,68},{40,8},{44,76},{48,1... | collective-permute-start | bytes 24584 | tf_op jit(solution)/shard_map/ppermute | solution.py:69
  29.2 0.1 dynamic-slice_bitcast_fusion.refs_8_
  29.3 2.7 %share.2.p_ref = bf16[4096,512]{1,0:T(8,128)(2,1)S(1)} custom-call(s32[4]{0:T(128)S(1)} %pad_add_fusion.place, bf16[4096,2048]{1,0:T(8,128)(2,1)} %p_ref.5), custom_call_target="tpu_custom_call" | custom-call | bytes 8388608 | tf_op jit(solution)/shard_map/share/pallas_call | solution.py:167
  32.0 0.0 collective-permute-done.7
  32.1 0.0 copy-start.1
  32.1 0.0 collective-permute-done.6.refs_3_
  32.1 0.0 collective-permute-done.4.refs_4_
  32.1 1.4 %lag.1.lagged.refs_0_ = bf16[16,256,512]{2,1,0:T(8,128)(2,1)S(1)} custom-call(s32[4]{0:T(128)S(1)} %pad_add_fusion.place, bf16[8,32,512]{2,1,0:T(8,128)(2,1)S(1)} %bitcast.43, bf16[8,32,512]{2,1,0:T(8,128)(2,1)S(1)} %collective-permute-done.refs_0_, bf16[8,32,512]{2,1,0:T(8,128)(2,1)S(1)} %collective-permute-done.1.refs_1_, ...), custom_call_target="tpu_custom_call" | custom-call | flops 1048576 | bytes 1048576 | tf_op jit(solution)/shard_map/lag/pallas_call | solution.py:103
  33.5 2.8 %collective-permute-start.9 = (bf16[2064,128]{1,0:T(8,128)(2,1)S(1)}, bf16[2064,128]{1,0:T(8,128)(2,1)S(1)}, u32[]{:S(2)}, u32[]{:S(2)}) collective-permute-start(bf16[2064,128]{1,0:T(8,128)(2,1)S(1)} %get-tuple-element.51), channel_id=1, source_target_pairs={{0,2},{1,3},{2,0},{3,1},{4,6},{5,7},{6,4},{7,5},{8,10},{9,11},{10,... | collective-permute-start | bytes 1585160 | tf_op jit(solution)/shard_map/ppermute | solution.py:77
  36.3 0.0 collective-permute-start.10
  36.3 0.7 collective-permute-start.11
  37.0 11.4 %feats.2 = (bf16[3072,512]{1,0:T(8,128)(2,1)S(1)}, bf16[3072,512]{1,0:T(8,128)(2,1)S(1)}) custom-call(s32[4]{0:T(128)S(1)} %pad_add_fusion.place, bf16[16,256,512]{2,1,0:T(8,128)(2,1)S(1)} %lag.1.lagged.refs_0_, bf16[4096,512]{1,0:T(8,128)(2,1)S(1)} %share.2.p_ref, f32[1,2048]{1,0:T(1,128)S(1)} %bitcast.48), custom_call_target="tpu_custom_call" | custom-call | flops 12884901888 | bytes 4194304 | tf_op jit(solution)/shard_map/feats/pallas_call | solution.py:206
  48.5 0.0 collective-permute-done.9.refs_4_
  48.5 0.4 collective-permute-start.12
  48.9 2.7 %share.3.p_ref = bf16[4096,512]{1,0:T(8,128)(2,1)S(1)} custom-call(s32[4]{0:T(128)S(1)} %pad_add_fusion.place, bf16[4096,2048]{1,0:T(8,128)(2,1)} %p_ref.5), custom_call_target="tpu_custom_call" | custom-call | bytes 8388608 | tf_op jit(solution)/shard_map/share/pallas_call | solution.py:167
  51.7 11.6 %window.1 = (bf16[512,3072]{1,0:T(8,128)(2,1)S(1)}, bf16[512,3072]{1,0:T(8,128)(2,1)S(1)}) custom-call(s32[4]{0:T(128)S(1)} %pad_add_fusion.place, bf16[16,256,512]{2,1,0:T(8,128)(2,1)S(1)} %lag.1.lagged.refs_0_, bf16[4096,128]{1,0:T(8,128)(2,1)S(1)} %get-tuple-element.50.refs_1_, bf16[2064,128]{1,0:T(8,128)(2,1)S(1)} %collective-permute-done.5.refs_2_, ...), custom_call_target="tpu_custom_call" | custom-call | flops 8589934592 | bytes 8388608 | tf_op jit(solution)/shard_map/window/pallas_call | solution.py:272
  63.3 16.4 %products.2 = (f32[2,128,512]{2,1,0:T(8,128)S(1)}, bf16[2,128,512]{2,1,0:T(8,128)(2,1)S(1)}, bf16[2,128,512]{2,1,0:T(8,128)(2,1)S(1)}, bf16[2,128,512]{2,1,0:T(8,128)(2,1)S(1)}) custom-call(bf16[512,3072]{1,0:T(8,128)(2,1)S(1)} %get-tuple-element.65.wh_ref, bf16[512,3072]{1,0:T(8,128)(2,1)S(1)} %get-tuple-element.66.wl_ref, ...), custom_call_target="tpu_custom_call" | custom-call | flops 1048576 | bytes 1048576 | tf_op jit(solution)/shard_map/products/pallas_call | solution.py:304
  79.7 1.2 %collective-permute-start.13 = (bf16[2,128,512]{2,1,0:T(8,128)(2,1)S(1)}, bf16[2,128,512]{2,1,0:T(8,128)(2,1)S(1)}, u32[]{:S(2)}, u32[]{:S(2)}) collective-permute-start(bf16[2,128,512]{2,1,0:T(8,128)(2,1)S(1)} %get-tuple-element.68), channel_id=1, source_target_pairs={{0,32},{4,36},{8,40},{12,44},{16,48},{20,52},{24,56},{28,60},{32,6... | collective-permute-start | bytes 786440 | tf_op jit(solution)/shard_map/ppermute | solution.py:69
  81.0 1.5 %collective-permute-start.14 = (bf16[2,128,512]{2,1,0:T(8,128)(2,1)S(1)}, bf16[2,128,512]{2,1,0:T(8,128)(2,1)S(1)}, u32[]{:S(2)}, u32[]{:S(2)}) collective-permute-start(bf16[2,128,512]{2,1,0:T(8,128)(2,1)S(1)} %get-tuple-element.69), channel_id=1, source_target_pairs={{0,96},{4,100},{8,104},{12,108},{16,112},{20,116},{24,120},{28,124... | collective-permute-start | bytes 786440 | tf_op jit(solution)/shard_map/ppermute | solution.py:69
  82.5 1.0 collective-permute-start.15
  83.5 11.4 %feats.3 = (bf16[3072,512]{1,0:T(8,128)(2,1)S(1)}, bf16[3072,512]{1,0:T(8,128)(2,1)S(1)}) custom-call(s32[4]{0:T(128)S(1)} %pad_add_fusion.place, bf16[16,256,512]{2,1,0:T(8,128)(2,1)S(1)} %lag.1.lagged.refs_0_, bf16[4096,512]{1,0:T(8,128)(2,1)S(1)} %share.3.p_ref, f32[1,2048]{1,0:T(1,128)S(1)} %bitcast.49), custom_call_target="tpu_custom_call" | custom-call | flops 12884901888 | bytes 4194304 | tf_op jit(solution)/shard_map/feats/pallas_call | solution.py:206
  95.0 6.2 %products.3 = (f32[2,128,512]{2,1,0:T(8,128)S(1)}, bf16[2,128,512]{2,1,0:T(8,128)(2,1)S(1)}, bf16[2,128,512]{2,1,0:T(8,128)(2,1)S(1)}, bf16[2,128,512]{2,1,0:T(8,128)(2,1)S(1)}) custom-call(bf16[512,3072]{1,0:T(8,128)(2,1)S(1)} %get-tuple-element.65.wh_ref, bf16[512,3072]{1,0:T(8,128)(2,1)S(1)} %get-tuple-element.66.wl_ref, ...), custom_call_target="tpu_custom_call" | custom-call | flops 1048576 | bytes 1048576 | tf_op jit(solution)/shard_map/products/pallas_call | solution.py:304
  101.2 0.2 collective-permute-start.17
  101.4 2.6 %collective-permute-start.18 = (bf16[2,128,512]{2,1,0:T(8,128)(2,1)S(1)}, bf16[2,128,512]{2,1,0:T(8,128)(2,1)S(1)}, u32[]{:S(2)}, u32[]{:S(2)}) collective-permute-start(bf16[2,128,512]{2,1,0:T(8,128)(2,1)S(1)} %get-tuple-element.88), channel_id=1, source_target_pairs={{0,96},{4,100},{8,104},{12,108},{16,112},{20,116},{24,120},{28,124... | collective-permute-start | bytes 786440 | tf_op jit(solution)/shard_map/ppermute | solution.py:69
  104.0 0.7 collective-permute-start.19
  104.7 0.6 fusion.3
  105.4 2.3 %collective-permute-start.16 = (f32[2,64,512]{2,1,0:T(8,128)S(1)}, f32[2,64,512]{2,1,0:T(8,128)S(1)}, u32[]{:S(2)}, u32[]{:S(2)}) collective-permute-start(f32[2,64,512]{2,1,0:T(8,128)S(1)} %get-tuple-element.92), channel_id=1, source_target_pairs={{0,4},{4,0},{8,12},{12,8},{16,20},{20,16},{24,28},{28,24},{32,36},... | collective-permute-start | bytes 786440 | tf_op jit(solution)/shard_map/ppermute | solution.py:69
  107.6 2.4 %collective-permute-done.17 = bf16[2,128,512]{2,1,0:T(8,128)(2,1)S(1)} collective-permute-done((bf16[2,128,512]{2,1,0:T(8,128)(2,1)S(1)}, bf16[2,128,512]{2,1,0:T(8,128)(2,1)S(1)}, u32[]{:S(2)}, u32[]{:S(2)}) %collective-permute-start.17) | collective-permute-done | bytes 262176 | tf_op jit(solution)/shard_map/ppermute | solution.py:69
  110.0 4.6 %collective-permute-done.19 = bf16[2,128,512]{2,1,0:T(8,128)(2,1)S(1)} collective-permute-done((bf16[2,128,512]{2,1,0:T(8,128)(2,1)S(1)}, bf16[2,128,512]{2,1,0:T(8,128)(2,1)S(1)}, u32[]{:S(2)}, u32[]{:S(2)}) %collective-permute-start.19) | collective-permute-done | bytes 262176 | tf_op jit(solution)/shard_map/ppermute | solution.py:69
  114.6 0.6 fusion.7
  115.3 2.3 %collective-permute-start.20 = (f32[2,64,512]{2,1,0:T(8,128)S(1)}, f32[2,64,512]{2,1,0:T(8,128)S(1)}, u32[]{:S(2)}, u32[]{:S(2)}) collective-permute-start(f32[2,64,512]{2,1,0:T(8,128)S(1)} %get-tuple-element.94), channel_id=1, source_target_pairs={{0,4},{4,0},{8,12},{12,8},{16,20},{20,16},{24,28},{28,24},{32,36},... | collective-permute-start | bytes 786440 | tf_op jit(solution)/shard_map/ppermute | solution.py:69
  117.6 1.2 collective-permute-done.20
  118.8 0.2 maximum_select_fusion
  118.9 1.1 fusion.8
  (27 shorter events, 0.3 us)
Async XLA Ops:
  1.7 8.9 %collective-permute-start.3 = (bf16[8,32,512]{2,1,0:T(8,128)(2,1)S(1)}, bf16[8,32,512]{2,1,0:T(8,128)(2,1)S(1)}, u32[]{:S(2)}, u32[]{:S(2)}) collective-permute-start(bf16[8,32,512]{2,1,0:T(8,128)(2,1)S(1)} %bitcast.38), channel_id=1, source_target_pairs={{0,4},{4,0},{8,12},{12,8},{16,20},{20,16},{24,28},{28,24},{32,36},... | collective-permute-start | bytes 786440 | tf_op jit(solution)/shard_map/ppermute | solution.py:69
  3.2 15.1 %collective-permute-start.2 = (bf16[8,32,512]{2,1,0:T(8,128)(2,1)S(1)}, bf16[8,32,512]{2,1,0:T(8,128)(2,1)S(1)}, u32[]{:S(2)}, u32[]{:S(2)}) collective-permute-start(bf16[8,32,512]{2,1,0:T(8,128)(2,1)S(1)} %bitcast.39), channel_id=1, source_target_pairs={{0,24},{4,28},{8,0},{12,4},{16,8},{20,12},{24,16},{28,20},{32,56},... | collective-permute-start | bytes 786440 | tf_op jit(solution)/shard_map/ppermute | solution.py:69
  7.0 11.3 %collective-permute-start.1 = (bf16[8,32,512]{2,1,0:T(8,128)(2,1)S(1)}, bf16[8,32,512]{2,1,0:T(8,128)(2,1)S(1)}, u32[]{:S(2)}, u32[]{:S(2)}) collective-permute-start(bf16[8,32,512]{2,1,0:T(8,128)(2,1)S(1)} %bitcast.40), channel_id=1, source_target_pairs={{0,16},{4,20},{8,24},{12,28},{16,0},{20,4},{24,8},{28,12},{32,48},... | collective-permute-start | bytes 786440 | tf_op jit(solution)/shard_map/ppermute | solution.py:69
  7.0 14.8 %collective-permute-start = (bf16[8,32,512]{2,1,0:T(8,128)(2,1)S(1)}, bf16[8,32,512]{2,1,0:T(8,128)(2,1)S(1)}, u32[]{:S(2)}, u32[]{:S(2)}) collective-permute-start(bf16[8,32,512]{2,1,0:T(8,128)(2,1)S(1)} %bitcast.41), channel_id=1, source_target_pairs={{0,8},{4,12},{8,16},{12,20},{16,24},{20,28},{24,0},{28,4},{32,40},... | collective-permute-start | bytes 786440 | tf_op jit(solution)/shard_map/ppermute | solution.py:69
  7.8 0.7 copy-start
  10.5 21.6 %collective-permute-start.6 = (bf16[2064,128]{1,0:T(8,128)(2,1)S(1)}, bf16[2064,128]{1,0:T(8,128)(2,1)S(1)}, u32[]{:S(2)}, u32[]{:S(2)}) collective-permute-start(bf16[2064,128]{1,0:T(8,128)(2,1)S(1)} %get-tuple-element.51), channel_id=1, source_target_pairs={{0,3},{1,0},{2,1},{3,2},{4,7},{5,4},{6,5},{7,6},{8,11},{9,8},{10,9... | collective-permute-start | bytes 1585160 | tf_op jit(solution)/shard_map/ppermute | solution.py:77
  13.1 19.0 %collective-permute-start.5 = (bf16[2064,128]{1,0:T(8,128)(2,1)S(1)}, bf16[2064,128]{1,0:T(8,128)(2,1)S(1)}, u32[]{:S(2)}, u32[]{:S(2)}) collective-permute-start(bf16[2064,128]{1,0:T(8,128)(2,1)S(1)} %get-tuple-element.51), channel_id=1, source_target_pairs={{0,1},{1,2},{2,3},{3,0},{4,5},{5,6},{6,7},{7,4},{8,9},{9,10},{10,1... | collective-permute-start | bytes 1585160 | tf_op jit(solution)/shard_map/ppermute | solution.py:77
  21.9 10.2 %collective-permute-start.4 = (bf16[3,8,32,512]{3,2,1,0:T(8,128)(2,1)S(1)}, bf16[3,8,32,512]{3,2,1,0:T(8,128)(2,1)S(1)}, u32[]{:S(2)}, u32[]{:S(2)}) collective-permute-start(bf16[3,8,32,512]{3,2,1,0:T(8,128)(2,1)S(1)} %pad_maximum_fusion), channel_id=1, source_target_pairs={{0,4},{4,0},{8,12},{12,8},{16,20},{20,16},{24,28},{28,24},{32,36},... | collective-permute-start | bytes 2359304 | tf_op jit(solution)/shard_map/ppermute | solution.py:69
  22.9 9.2 %collective-permute-start.8 = (bf16[8,512]{1,0:T(8,128)(2,1)S(1)}, bf16[8,512]{1,0:T(8,128)(2,1)S(1)}, u32[]{:S(2)}, u32[]{:S(2)}) collective-permute-start(bf16[8,512]{1,0:T(8,128)(2,1)S(1)} %fusion.13), channel_id=1, source_target_pairs={{4,32},{12,40},{20,48},{28,56},{32,4},{36,64},{40,12},{44,72},{48,... | collective-permute-start | bytes 24584 | tf_op jit(solution)/shard_map/ppermute | solution.py:69
  26.0 6.1 %collective-permute-start.7 = (bf16[8,512]{1,0:T(8,128)(2,1)S(1)}, bf16[8,512]{1,0:T(8,128)(2,1)S(1)}, u32[]{:S(2)}, u32[]{:S(2)}) collective-permute-start(bf16[8,512]{1,0:T(8,128)(2,1)S(1)} %fusion.13), channel_id=1, source_target_pairs={{4,36},{12,44},{20,52},{28,60},{32,0},{36,68},{40,8},{44,76},{48,1... | collective-permute-start | bytes 24584 | tf_op jit(solution)/shard_map/ppermute | solution.py:69
  32.1 5.0 %copy-start.1 = (f32[2048]{0:T(1024)S(1)}, f32[2048]{0:T(1024)}, u32[]{:S(2)}) copy-start(f32[2048]{0:T(1024)} %param.5) | copy-start | bytes 24580
  33.5 15.0 %collective-permute-start.9 = (bf16[2064,128]{1,0:T(8,128)(2,1)S(1)}, bf16[2064,128]{1,0:T(8,128)(2,1)S(1)}, u32[]{:S(2)}, u32[]{:S(2)}) collective-permute-start(bf16[2064,128]{1,0:T(8,128)(2,1)S(1)} %get-tuple-element.51), channel_id=1, source_target_pairs={{0,2},{1,3},{2,0},{3,1},{4,6},{5,7},{6,4},{7,5},{8,10},{9,11},{10,... | collective-permute-start | bytes 1585160 | tf_op jit(solution)/shard_map/ppermute | solution.py:77
  36.3 15.3 %collective-permute-start.10 = (bf16[2064,128]{1,0:T(8,128)(2,1)S(1)}, bf16[2064,128]{1,0:T(8,128)(2,1)S(1)}, u32[]{:S(2)}, u32[]{:S(2)}) collective-permute-start(bf16[2064,128]{1,0:T(8,128)(2,1)S(1)} %collective-permute-done.5.refs_2_), channel_id=1, source_target_pairs={{0,4},{4,0},{8,12},{12,8},{16,20},{20,16},{24,28},{28,24},{32,36},... | collective-permute-start | bytes 1585160 | tf_op jit(solution)/shard_map/ppermute | solution.py:69
  36.3 15.3 %collective-permute-start.11 = (bf16[2064,128]{1,0:T(8,128)(2,1)S(1)}, bf16[2064,128]{1,0:T(8,128)(2,1)S(1)}, u32[]{:S(2)}, u32[]{:S(2)}) collective-permute-start(bf16[2064,128]{1,0:T(8,128)(2,1)S(1)} %collective-permute-done.6.refs_3_), channel_id=1, source_target_pairs={{0,4},{4,0},{8,12},{12,8},{16,20},{20,16},{24,28},{28,24},{32,36},... | collective-permute-start | bytes 1585160 | tf_op jit(solution)/shard_map/ppermute | solution.py:69
  48.5 3.2 %collective-permute-start.12 = (bf16[2064,128]{1,0:T(8,128)(2,1)S(1)}, bf16[2064,128]{1,0:T(8,128)(2,1)S(1)}, u32[]{:S(2)}, u32[]{:S(2)}) collective-permute-start(bf16[2064,128]{1,0:T(8,128)(2,1)S(1)} %collective-permute-done.9.refs_4_), channel_id=1, source_target_pairs={{0,4},{4,0},{8,12},{12,8},{16,20},{20,16},{24,28},{28,24},{32,36},... | collective-permute-start | bytes 1585160 | tf_op jit(solution)/shard_map/ppermute | solution.py:69
  79.7 21.5 %collective-permute-start.13 = (bf16[2,128,512]{2,1,0:T(8,128)(2,1)S(1)}, bf16[2,128,512]{2,1,0:T(8,128)(2,1)S(1)}, u32[]{:S(2)}, u32[]{:S(2)}) collective-permute-start(bf16[2,128,512]{2,1,0:T(8,128)(2,1)S(1)} %get-tuple-element.68), channel_id=1, source_target_pairs={{0,32},{4,36},{8,40},{12,44},{16,48},{20,52},{24,56},{28,60},{32,6... | collective-permute-start | bytes 786440 | tf_op jit(solution)/shard_map/ppermute | solution.py:69
  81.0 20.2 %collective-permute-start.14 = (bf16[2,128,512]{2,1,0:T(8,128)(2,1)S(1)}, bf16[2,128,512]{2,1,0:T(8,128)(2,1)S(1)}, u32[]{:S(2)}, u32[]{:S(2)}) collective-permute-start(bf16[2,128,512]{2,1,0:T(8,128)(2,1)S(1)} %get-tuple-element.69), channel_id=1, source_target_pairs={{0,96},{4,100},{8,104},{12,108},{16,112},{20,116},{24,120},{28,124... | collective-permute-start | bytes 786440 | tf_op jit(solution)/shard_map/ppermute | solution.py:69
  82.5 18.8 %collective-permute-start.15 = (bf16[2,128,512]{2,1,0:T(8,128)(2,1)S(1)}, bf16[2,128,512]{2,1,0:T(8,128)(2,1)S(1)}, u32[]{:S(2)}, u32[]{:S(2)}) collective-permute-start(bf16[2,128,512]{2,1,0:T(8,128)(2,1)S(1)} %get-tuple-element.70), channel_id=1, source_target_pairs={{0,64},{4,68},{8,72},{12,76},{16,80},{20,84},{24,88},{28,92},{32,9... | collective-permute-start | bytes 786440 | tf_op jit(solution)/shard_map/ppermute | solution.py:69
  101.2 8.8 %collective-permute-start.17 = (bf16[2,128,512]{2,1,0:T(8,128)(2,1)S(1)}, bf16[2,128,512]{2,1,0:T(8,128)(2,1)S(1)}, u32[]{:S(2)}, u32[]{:S(2)}) collective-permute-start(bf16[2,128,512]{2,1,0:T(8,128)(2,1)S(1)} %get-tuple-element.87), channel_id=1, source_target_pairs={{0,32},{4,36},{8,40},{12,44},{16,48},{20,52},{24,56},{28,60},{32,6... | collective-permute-start | bytes 786440 | tf_op jit(solution)/shard_map/ppermute | solution.py:69
  101.4 8.6 %collective-permute-start.18 = (bf16[2,128,512]{2,1,0:T(8,128)(2,1)S(1)}, bf16[2,128,512]{2,1,0:T(8,128)(2,1)S(1)}, u32[]{:S(2)}, u32[]{:S(2)}) collective-permute-start(bf16[2,128,512]{2,1,0:T(8,128)(2,1)S(1)} %get-tuple-element.88), channel_id=1, source_target_pairs={{0,96},{4,100},{8,104},{12,108},{16,112},{20,116},{24,120},{28,124... | collective-permute-start | bytes 786440 | tf_op jit(solution)/shard_map/ppermute | solution.py:69
  104.0 10.6 %collective-permute-start.19 = (bf16[2,128,512]{2,1,0:T(8,128)(2,1)S(1)}, bf16[2,128,512]{2,1,0:T(8,128)(2,1)S(1)}, u32[]{:S(2)}, u32[]{:S(2)}) collective-permute-start(bf16[2,128,512]{2,1,0:T(8,128)(2,1)S(1)} %get-tuple-element.89), channel_id=1, source_target_pairs={{0,64},{4,68},{8,72},{12,76},{16,80},{20,84},{24,88},{28,92},{32,9... | collective-permute-start | bytes 786440 | tf_op jit(solution)/shard_map/ppermute | solution.py:69
  105.4 12.3 %collective-permute-start.16 = (f32[2,64,512]{2,1,0:T(8,128)S(1)}, f32[2,64,512]{2,1,0:T(8,128)S(1)}, u32[]{:S(2)}, u32[]{:S(2)}) collective-permute-start(f32[2,64,512]{2,1,0:T(8,128)S(1)} %get-tuple-element.92), channel_id=1, source_target_pairs={{0,4},{4,0},{8,12},{12,8},{16,20},{20,16},{24,28},{28,24},{32,36},... | collective-permute-start | bytes 786440 | tf_op jit(solution)/shard_map/ppermute | solution.py:69
  115.3 3.5 %collective-permute-start.20 = (f32[2,64,512]{2,1,0:T(8,128)S(1)}, f32[2,64,512]{2,1,0:T(8,128)S(1)}, u32[]{:S(2)}, u32[]{:S(2)}) collective-permute-start(f32[2,64,512]{2,1,0:T(8,128)S(1)} %get-tuple-element.94), channel_id=1, source_target_pairs={{0,4},{4,0},{8,12},{12,8},{16,20},{20,16},{24,28},{28,24},{32,36},... | collective-permute-start | bytes 786440 | tf_op jit(solution)/shard_map/ppermute | solution.py:69

commit v2 on v1

--- a/solution.py
+++ b/solution.py
@@ -353,7 +353,7 @@
     near = [around(piece, by) for by in (1, 3)]
     lagged = lag(place, own, other, after(others, near), edge)
     swapped = [swap(v) for v in after(near, lagged)]
-    near = [*near, around(after(piece, lagged), 2)]
+    near = [*near, around(after(piece, near), 2)]
 
     def feats(first, blocks, share, *others):
         return feats_of(first, blocks, place, after(lagged, *others), share, phases)

time: 119 us -> 119 us (level)
  transfers between devices with their start and end apart: 21 -> 21, of which waited for: 5 -> 5; matrix products, arithmetic and copies ran while one was open for 1% -> 1% of each run, Pallas kernels for 30% -> 32%
where the time goes in v2:
time: 119 us; the launch traced here: 120 us
  Pallas kernels  65.9 us (55%)
  starting transfers between devices  31.5 us (26%)
  waiting for transfers between devices  16.7 us (14%)
  other arithmetic  2.9 us (2%)
  local copies, waits for them, and re-layouts  1.84 us (2%)
    ppermute x18, starting transfers between devices, move(): return lax.ppermute(value, 'tm', pairs)  26.1 us
    pallas_call x2, Pallas kernels, feats_of(): pl.pallas_call(functools.partial(feats_kernel, first), out_shape=(out, ou...  22.9 us
    pallas_call x2, Pallas kernels, products_of(): pl.pallas_call(products_kernel, out_shape=[jax.ShapeDtypeStruct((2, part,...  22.7 us
    ppermute x18, waiting for transfers between devices, move(): return lax.ppermute(value, 'tm', pairs)  16.7 us
    pallas_call x1, Pallas kernels, window_of(): pl.pallas_call(window_kernel, out_shape=(out, out), in_specs=[pl.BlockSpe...  11.6 us
    pallas_call x2, Pallas kernels, share_of(): pl.pallas_call(functools.partial(share_kernel, part), out_shape=jax.Shape...  5.48 us
    ppermute x3, starting transfers between devices, around(): return lax.ppermute(value, 'feat', [(i, (i + by) % 4) for i in range(4)])  5.37 us
  transfers between devices with their start and end apart: 21, of which 5 were waited for; matrix products, arithmetic and copies ran while one was open for 1% of the time, Pallas kernels for 32%

profile of v2, /device:TPU:1, one launch (start us, length us, event | category | flops | bytes accessed | tf_op | source)
XLA Modules:
  0.0 120.0 jit_solution(4129057107004287822)
XLA Ops:
  0.6 1.0 copy.39
  1.7 1.5 %collective-permute-start.3 = (bf16[8,32,512]{2,1,0:T(8,128)(2,1)S(1)}, bf16[8,32,512]{2,1,0:T(8,128)(2,1)S(1)}, u32[]{:S(2)}, u32[]{:S(2)}) collective-permute-start(bf16[8,32,512]{2,1,0:T(8,128)(2,1)S(1)} %bitcast.38), channel_id=1, source_target_pairs={{0,4},{4,0},{8,12},{12,8},{16,20},{20,16},{24,28},{28,24},{32,36},... | collective-permute-start | bytes 786440 | tf_op jit(solution)/shard_map/ppermute | solution.py:69
  3.2 3.9 %collective-permute-start.2 = (bf16[8,32,512]{2,1,0:T(8,128)(2,1)S(1)}, bf16[8,32,512]{2,1,0:T(8,128)(2,1)S(1)}, u32[]{:S(2)}, u32[]{:S(2)}) collective-permute-start(bf16[8,32,512]{2,1,0:T(8,128)(2,1)S(1)} %bitcast.39), channel_id=1, source_target_pairs={{0,24},{4,28},{8,0},{12,4},{16,8},{20,12},{24,16},{28,20},{32,56},... | collective-permute-start | bytes 786440 | tf_op jit(solution)/shard_map/ppermute | solution.py:69
  7.0 0.0 collective-permute-start.1
  7.0 0.7 collective-permute-start
  7.8 0.1 pad_add_fusion.place
  7.8 0.7 copy-done
  8.5 2.0 %prepare.1 = (bf16[2064,128]{1,0:T(8,128)(2,1)S(1)}, bf16[4096,128]{1,0:T(8,128)(2,1)S(1)}) custom-call(s32[4]{0:T(128)S(1)} %pad_add_fusion.place, bf16[4096,2048]{1,0:T(8,128)(2,1)} %p_ref.5, f32[1,2048]{1,0:T(1,128)S(1)} %bitcast.47), custom_call_target="tpu_custom_call" | custom-call | bytes 3145728 | tf_op jit(solution)/shard_map/prepare/pallas_call | solution.py:138
  10.5 2.5 %collective-permute-start.6 = (bf16[2064,128]{1,0:T(8,128)(2,1)S(1)}, bf16[2064,128]{1,0:T(8,128)(2,1)S(1)}, u32[]{:S(2)}, u32[]{:S(2)}) collective-permute-start(bf16[2064,128]{1,0:T(8,128)(2,1)S(1)} %get-tuple-element.51), channel_id=1, source_target_pairs={{0,3},{1,0},{2,1},{3,2},{4,7},{5,4},{6,5},{7,6},{8,11},{9,8},{10,9... | collective-permute-start | bytes 1585160 | tf_op jit(solution)/shard_map/ppermute | solution.py:77
  13.1 5.2 %collective-permute-done.2.refs_2_ = bf16[8,32,512]{2,1,0:T(8,128)(2,1)S(1)} collective-permute-done((bf16[8,32,512]{2,1,0:T(8,128)(2,1)S(1)}, bf16[8,32,512]{2,1,0:T(8,128)(2,1)S(1)}, u32[]{:S(2)}, u32[]{:S(2)}) %collective-permute-start.2) | collective-permute-done | bytes 262176 | tf_op jit(solution)/shard_map/ppermute | solution.py:69
  18.3 0.0 collective-permute-done.1.refs_1_
  18.4 3.5 %collective-permute-done.refs_0_ = bf16[8,32,512]{2,1,0:T(8,128)(2,1)S(1)} collective-permute-done((bf16[8,32,512]{2,1,0:T(8,128)(2,1)S(1)}, bf16[8,32,512]{2,1,0:T(8,128)(2,1)S(1)}, u32[]{:S(2)}, u32[]{:S(2)}) %collective-permute-start) | collective-permute-done | bytes 262176 | tf_op jit(solution)/shard_map/ppermute | solution.py:69
  21.8 0.1 pad_maximum_fusion
  21.9 0.8 collective-permute-start.4
  22.9 3.1 %collective-permute-start.8 = (bf16[8,512]{1,0:T(8,128)(2,1)S(1)}, bf16[8,512]{1,0:T(8,128)(2,1)S(1)}, u32[]{:S(2)}, u32[]{:S(2)}) collective-permute-start(bf16[8,512]{1,0:T(8,128)(2,1)S(1)} %fusion.13), channel_id=1, source_target_pairs={{4,32},{12,40},{20,48},{28,56},{32,4},{36,64},{40,12},{44,72},{48,... | collective-permute-start | bytes 24584 | tf_op jit(solution)/shard_map/ppermute | solution.py:69
  26.0 3.2 %collective-permute-start.7 = (bf16[8,512]{1,0:T(8,128)(2,1)S(1)}, bf16[8,512]{1,0:T(8,128)(2,1)S(1)}, u32[]{:S(2)}, u32[]{:S(2)}) collective-permute-start(bf16[8,512]{1,0:T(8,128)(2,1)S(1)} %fusion.13), channel_id=1, source_target_pairs={{4,36},{12,44},{20,52},{28,60},{32,0},{36,68},{40,8},{44,76},{48,1... | collective-permute-start | bytes 24584 | tf_op jit(solution)/shard_map/ppermute | solution.py:69
  29.2 0.1 dynamic-slice_bitcast_fusion.refs_8_
  29.3 2.7 %share.2.p_ref = bf16[4096,512]{1,0:T(8,128)(2,1)S(1)} custom-call(s32[4]{0:T(128)S(1)} %pad_add_fusion.place, bf16[4096,2048]{1,0:T(8,128)(2,1)} %p_ref.5), custom_call_target="tpu_custom_call" | custom-call | bytes 8388608 | tf_op jit(solution)/shard_map/share/pallas_call | solution.py:167
  32.0 0.0 collective-permute-done.8
  32.1 0.0 copy-start.1
  32.1 0.0 collective-permute-done.6.refs_3_
  32.1 0.0 collective-permute-done.5.refs_2_
  32.1 2.8 %collective-permute-start.9 = (bf16[2064,128]{1,0:T(8,128)(2,1)S(1)}, bf16[2064,128]{1,0:T(8,128)(2,1)S(1)}, u32[]{:S(2)}, u32[]{:S(2)}) collective-permute-start(bf16[2064,128]{1,0:T(8,128)(2,1)S(1)} %get-tuple-element.51), channel_id=1, source_target_pairs={{0,2},{1,3},{2,0},{3,1},{4,6},{5,7},{6,4},{7,5},{8,10},{9,11},{10,... | collective-permute-start | bytes 1585160 | tf_op jit(solution)/shard_map/ppermute | solution.py:77
  34.9 1.4 %lag.1.lagged.refs_0_ = bf16[16,256,512]{2,1,0:T(8,128)(2,1)S(1)} custom-call(s32[4]{0:T(128)S(1)} %pad_add_fusion.place, bf16[8,32,512]{2,1,0:T(8,128)(2,1)S(1)} %bitcast.43, bf16[8,32,512]{2,1,0:T(8,128)(2,1)S(1)} %collective-permute-done.refs_0_, bf16[8,32,512]{2,1,0:T(8,128)(2,1)S(1)} %collective-permute-done.1.refs_1_, ...), custom_call_target="tpu_custom_call" | custom-call | flops 1048576 | bytes 1048576 | tf_op jit(solution)/shard_map/lag/pallas_call | solution.py:103
  36.3 0.1 collective-permute-start.10
  36.4 0.7 collective-permute-start.11
  37.1 11.4 %feats.2 = (bf16[3072,512]{1,0:T(8,128)(2,1)S(1)}, bf16[3072,512]{1,0:T(8,128)(2,1)S(1)}) custom-call(s32[4]{0:T(128)S(1)} %pad_add_fusion.place, bf16[16,256,512]{2,1,0:T(8,128)(2,1)S(1)} %lag.1.lagged.refs_0_, bf16[4096,512]{1,0:T(8,128)(2,1)S(1)} %share.2.p_ref, f32[1,2048]{1,0:T(1,128)S(1)} %bitcast.48), custom_call_target="tpu_custom_call" | custom-call | flops 12884901888 | bytes 4194304 | tf_op jit(solution)/shard_map/feats/pallas_call | solution.py:206
  48.6 0.5 collective-permute-start.12
  49.1 2.7 %share.3.p_ref = bf16[4096,512]{1,0:T(8,128)(2,1)S(1)} custom-call(s32[4]{0:T(128)S(1)} %pad_add_fusion.place, bf16[4096,2048]{1,0:T(8,128)(2,1)} %p_ref.5), custom_call_target="tpu_custom_call" | custom-call | bytes 8388608 | tf_op jit(solution)/shard_map/share/pallas_call | solution.py:167
  51.8 11.6 %window.1 = (bf16[512,3072]{1,0:T(8,128)(2,1)S(1)}, bf16[512,3072]{1,0:T(8,128)(2,1)S(1)}) custom-call(s32[4]{0:T(128)S(1)} %pad_add_fusion.place, bf16[16,256,512]{2,1,0:T(8,128)(2,1)S(1)} %lag.1.lagged.refs_0_, bf16[4096,128]{1,0:T(8,128)(2,1)S(1)} %get-tuple-element.50.refs_1_, bf16[2064,128]{1,0:T(8,128)(2,1)S(1)} %collective-permute-done.5.refs_2_, ...), custom_call_target="tpu_custom_call" | custom-call | flops 8589934592 | bytes 8388608 | tf_op jit(solution)/shard_map/window/pallas_call | solution.py:272
  63.4 16.4 %products.2 = (f32[2,128,512]{2,1,0:T(8,128)S(1)}, bf16[2,128,512]{2,1,0:T(8,128)(2,1)S(1)}, bf16[2,128,512]{2,1,0:T(8,128)(2,1)S(1)}, bf16[2,128,512]{2,1,0:T(8,128)(2,1)S(1)}) custom-call(bf16[512,3072]{1,0:T(8,128)(2,1)S(1)} %get-tuple-element.65.wh_ref, bf16[512,3072]{1,0:T(8,128)(2,1)S(1)} %get-tuple-element.66.wl_ref, ...), custom_call_target="tpu_custom_call" | custom-call | flops 1048576 | bytes 1048576 | tf_op jit(solution)/shard_map/products/pallas_call | solution.py:304
  79.9 1.1 collective-permute-start.13
  80.9 1.7 %collective-permute-start.14 = (bf16[2,128,512]{2,1,0:T(8,128)(2,1)S(1)}, bf16[2,128,512]{2,1,0:T(8,128)(2,1)S(1)}, u32[]{:S(2)}, u32[]{:S(2)}) collective-permute-start(bf16[2,128,512]{2,1,0:T(8,128)(2,1)S(1)} %get-tuple-element.69), channel_id=1, source_target_pairs={{0,96},{4,100},{8,104},{12,108},{16,112},{20,116},{24,120},{28,124... | collective-permute-start | bytes 786440 | tf_op jit(solution)/shard_map/ppermute | solution.py:69
  82.6 0.7 collective-permute-start.15
  83.3 11.4 %feats.3 = (bf16[3072,512]{1,0:T(8,128)(2,1)S(1)}, bf16[3072,512]{1,0:T(8,128)(2,1)S(1)}) custom-call(s32[4]{0:T(128)S(1)} %pad_add_fusion.place, bf16[16,256,512]{2,1,0:T(8,128)(2,1)S(1)} %lag.1.lagged.refs_0_, bf16[4096,512]{1,0:T(8,128)(2,1)S(1)} %share.3.p_ref, f32[1,2048]{1,0:T(1,128)S(1)} %bitcast.49), custom_call_target="tpu_custom_call" | custom-call | flops 12884901888 | bytes 4194304 | tf_op jit(solution)/shard_map/feats/pallas_call | solution.py:206
  94.8 6.2 %products.3 = (f32[2,128,512]{2,1,0:T(8,128)S(1)}, bf16[2,128,512]{2,1,0:T(8,128)(2,1)S(1)}, bf16[2,128,512]{2,1,0:T(8,128)(2,1)S(1)}, bf16[2,128,512]{2,1,0:T(8,128)(2,1)S(1)}) custom-call(bf16[512,3072]{1,0:T(8,128)(2,1)S(1)} %get-tuple-element.65.wh_ref, bf16[512,3072]{1,0:T(8,128)(2,1)S(1)} %get-tuple-element.66.wl_ref, ...), custom_call_target="tpu_custom_call" | custom-call | flops 1048576 | bytes 1048576 | tf_op jit(solution)/shard_map/products/pallas_call | solution.py:304
  101.0 0.4 collective-permute-start.17
  101.4 2.3 %collective-permute-start.18 = (bf16[2,128,512]{2,1,0:T(8,128)(2,1)S(1)}, bf16[2,128,512]{2,1,0:T(8,128)(2,1)S(1)}, u32[]{:S(2)}, u32[]{:S(2)}) collective-permute-start(bf16[2,128,512]{2,1,0:T(8,128)(2,1)S(1)} %get-tuple-element.88), channel_id=1, source_target_pairs={{0,96},{4,100},{8,104},{12,108},{16,112},{20,116},{24,120},{28,124... | collective-permute-start | bytes 786440 | tf_op jit(solution)/shard_map/ppermute | solution.py:69
  103.8 1.0 collective-permute-start.19
  104.8 0.6 fusion.3
  105.5 2.1 %collective-permute-start.16 = (f32[2,64,512]{2,1,0:T(8,128)S(1)}, f32[2,64,512]{2,1,0:T(8,128)S(1)}, u32[]{:S(2)}, u32[]{:S(2)}) collective-permute-start(f32[2,64,512]{2,1,0:T(8,128)S(1)} %get-tuple-element.92), channel_id=1, source_target_pairs={{0,4},{4,0},{8,12},{12,8},{16,20},{20,16},{24,28},{28,24},{32,36},... | collective-permute-start | bytes 786440 | tf_op jit(solution)/shard_map/ppermute | solution.py:69
  107.7 1.8 %collective-permute-done.17 = bf16[2,128,512]{2,1,0:T(8,128)(2,1)S(1)} collective-permute-done((bf16[2,128,512]{2,1,0:T(8,128)(2,1)S(1)}, bf16[2,128,512]{2,1,0:T(8,128)(2,1)S(1)}, u32[]{:S(2)}, u32[]{:S(2)}) %collective-permute-start.17) | collective-permute-done | bytes 262176 | tf_op jit(solution)/shard_map/ppermute | solution.py:69
  109.5 5.0 %collective-permute-done.19 = bf16[2,128,512]{2,1,0:T(8,128)(2,1)S(1)} collective-permute-done((bf16[2,128,512]{2,1,0:T(8,128)(2,1)S(1)}, bf16[2,128,512]{2,1,0:T(8,128)(2,1)S(1)}, u32[]{:S(2)}, u32[]{:S(2)}) %collective-permute-start.19) | collective-permute-done | bytes 262176 | tf_op jit(solution)/shard_map/ppermute | solution.py:69
  114.5 0.6 fusion.7
  115.2 2.3 %collective-permute-start.20 = (f32[2,64,512]{2,1,0:T(8,128)S(1)}, f32[2,64,512]{2,1,0:T(8,128)S(1)}, u32[]{:S(2)}, u32[]{:S(2)}) collective-permute-start(f32[2,64,512]{2,1,0:T(8,128)S(1)} %get-tuple-element.94), channel_id=1, source_target_pairs={{0,4},{4,0},{8,12},{12,8},{16,20},{20,16},{24,28},{28,24},{32,36},... | collective-permute-start | bytes 786440 | tf_op jit(solution)/shard_map/ppermute | solution.py:69
  117.4 1.2 collective-permute-done.20
  118.6 0.2 maximum_select_fusion
  118.7 1.1 fusion.8
  (27 shorter events, 0.3 us)
Async XLA Ops:
  1.7 8.9 %collective-permute-start.3 = (bf16[8,32,512]{2,1,0:T(8,128)(2,1)S(1)}, bf16[8,32,512]{2,1,0:T(8,128)(2,1)S(1)}, u32[]{:S(2)}, u32[]{:S(2)}) collective-permute-start(bf16[8,32,512]{2,1,0:T(8,128)(2,1)S(1)} %bitcast.38), channel_id=1, source_target_pairs={{0,4},{4,0},{8,12},{12,8},{16,20},{20,16},{24,28},{28,24},{32,36},... | collective-permute-start | bytes 786440 | tf_op jit(solution)/shard_map/ppermute | solution.py:69
  3.2 15.1 %collective-permute-start.2 = (bf16[8,32,512]{2,1,0:T(8,128)(2,1)S(1)}, bf16[8,32,512]{2,1,0:T(8,128)(2,1)S(1)}, u32[]{:S(2)}, u32[]{:S(2)}) collective-permute-start(bf16[8,32,512]{2,1,0:T(8,128)(2,1)S(1)} %bitcast.39), channel_id=1, source_target_pairs={{0,24},{4,28},{8,0},{12,4},{16,8},{20,12},{24,16},{28,20},{32,56},... | collective-permute-start | bytes 786440 | tf_op jit(solution)/shard_map/ppermute | solution.py:69
  7.0 11.3 %collective-permute-start.1 = (bf16[8,32,512]{2,1,0:T(8,128)(2,1)S(1)}, bf16[8,32,512]{2,1,0:T(8,128)(2,1)S(1)}, u32[]{:S(2)}, u32[]{:S(2)}) collective-permute-start(bf16[8,32,512]{2,1,0:T(8,128)(2,1)S(1)} %bitcast.40), channel_id=1, source_target_pairs={{0,16},{4,20},{8,24},{12,28},{16,0},{20,4},{24,8},{28,12},{32,48},... | collective-permute-start | bytes 786440 | tf_op jit(solution)/shard_map/ppermute | solution.py:69
  7.0 14.8 %collective-permute-start = (bf16[8,32,512]{2,1,0:T(8,128)(2,1)S(1)}, bf16[8,32,512]{2,1,0:T(8,128)(2,1)S(1)}, u32[]{:S(2)}, u32[]{:S(2)}) collective-permute-start(bf16[8,32,512]{2,1,0:T(8,128)(2,1)S(1)} %bitcast.41), channel_id=1, source_target_pairs={{0,8},{4,12},{8,16},{12,20},{16,24},{20,28},{24,0},{28,4},{32,40},... | collective-permute-start | bytes 786440 | tf_op jit(solution)/shard_map/ppermute | solution.py:69
  7.8 0.7 copy-start
  10.5 21.6 %collective-permute-start.6 = (bf16[2064,128]{1,0:T(8,128)(2,1)S(1)}, bf16[2064,128]{1,0:T(8,128)(2,1)S(1)}, u32[]{:S(2)}, u32[]{:S(2)}) collective-permute-start(bf16[2064,128]{1,0:T(8,128)(2,1)S(1)} %get-tuple-element.51), channel_id=1, source_target_pairs={{0,3},{1,0},{2,1},{3,2},{4,7},{5,4},{6,5},{7,6},{8,11},{9,8},{10,9... | collective-permute-start | bytes 1585160 | tf_op jit(solution)/shard_map/ppermute | solution.py:77
  13.1 19.0 %collective-permute-start.5 = (bf16[2064,128]{1,0:T(8,128)(2,1)S(1)}, bf16[2064,128]{1,0:T(8,128)(2,1)S(1)}, u32[]{:S(2)}, u32[]{:S(2)}) collective-permute-start(bf16[2064,128]{1,0:T(8,128)(2,1)S(1)} %get-tuple-element.51), channel_id=1, source_target_pairs={{0,1},{1,2},{2,3},{3,0},{4,5},{5,6},{6,7},{7,4},{8,9},{9,10},{10,1... | collective-permute-start | bytes 1585160 | tf_op jit(solution)/shard_map/ppermute | solution.py:77
  21.9 13.0 %collective-permute-start.4 = (bf16[3,8,32,512]{3,2,1,0:T(8,128)(2,1)S(1)}, bf16[3,8,32,512]{3,2,1,0:T(8,128)(2,1)S(1)}, u32[]{:S(2)}, u32[]{:S(2)}) collective-permute-start(bf16[3,8,32,512]{3,2,1,0:T(8,128)(2,1)S(1)} %pad_maximum_fusion), channel_id=1, source_target_pairs={{0,4},{4,0},{8,12},{12,8},{16,20},{20,16},{24,28},{28,24},{32,36},... | collective-permute-start | bytes 2359304 | tf_op jit(solution)/shard_map/ppermute | solution.py:69
  22.9 9.2 %collective-permute-start.8 = (bf16[8,512]{1,0:T(8,128)(2,1)S(1)}, bf16[8,512]{1,0:T(8,128)(2,1)S(1)}, u32[]{:S(2)}, u32[]{:S(2)}) collective-permute-start(bf16[8,512]{1,0:T(8,128)(2,1)S(1)} %fusion.13), channel_id=1, source_target_pairs={{4,32},{12,40},{20,48},{28,56},{32,4},{36,64},{40,12},{44,72},{48,... | collective-permute-start | bytes 24584 | tf_op jit(solution)/shard_map/ppermute | solution.py:69
  26.0 6.1 %collective-permute-start.7 = (bf16[8,512]{1,0:T(8,128)(2,1)S(1)}, bf16[8,512]{1,0:T(8,128)(2,1)S(1)}, u32[]{:S(2)}, u32[]{:S(2)}) collective-permute-start(bf16[8,512]{1,0:T(8,128)(2,1)S(1)} %fusion.13), channel_id=1, source_target_pairs={{4,36},{12,44},{20,52},{28,60},{32,0},{36,68},{40,8},{44,76},{48,1... | collective-permute-start | bytes 24584 | tf_op jit(solution)/shard_map/ppermute | solution.py:69
  32.1 5.0 %copy-start.1 = (f32[2048]{0:T(1024)S(1)}, f32[2048]{0:T(1024)}, u32[]{:S(2)}) copy-start(f32[2048]{0:T(1024)} %param.5) | copy-start | bytes 24580
  32.1 16.4 %collective-permute-start.9 = (bf16[2064,128]{1,0:T(8,128)(2,1)S(1)}, bf16[2064,128]{1,0:T(8,128)(2,1)S(1)}, u32[]{:S(2)}, u32[]{:S(2)}) collective-permute-start(bf16[2064,128]{1,0:T(8,128)(2,1)S(1)} %get-tuple-element.51), channel_id=1, source_target_pairs={{0,2},{1,3},{2,0},{3,1},{4,6},{5,7},{6,4},{7,5},{8,10},{9,11},{10,... | collective-permute-start | bytes 1585160 | tf_op jit(solution)/shard_map/ppermute | solution.py:77
  36.3 15.5 %collective-permute-start.10 = (bf16[2064,128]{1,0:T(8,128)(2,1)S(1)}, bf16[2064,128]{1,0:T(8,128)(2,1)S(1)}, u32[]{:S(2)}, u32[]{:S(2)}) collective-permute-start(bf16[2064,128]{1,0:T(8,128)(2,1)S(1)} %collective-permute-done.5.refs_2_), channel_id=1, source_target_pairs={{0,4},{4,0},{8,12},{12,8},{16,20},{20,16},{24,28},{28,24},{32,36},... | collective-permute-start | bytes 1585160 | tf_op jit(solution)/shard_map/ppermute | solution.py:69
  36.4 15.4 %collective-permute-start.11 = (bf16[2064,128]{1,0:T(8,128)(2,1)S(1)}, bf16[2064,128]{1,0:T(8,128)(2,1)S(1)}, u32[]{:S(2)}, u32[]{:S(2)}) collective-permute-start(bf16[2064,128]{1,0:T(8,128)(2,1)S(1)} %collective-permute-done.6.refs_3_), channel_id=1, source_target_pairs={{0,4},{4,0},{8,12},{12,8},{16,20},{20,16},{24,28},{28,24},{32,36},... | collective-permute-start | bytes 1585160 | tf_op jit(solution)/shard_map/ppermute | solution.py:69
  48.6 3.3 %collective-permute-start.12 = (bf16[2064,128]{1,0:T(8,128)(2,1)S(1)}, bf16[2064,128]{1,0:T(8,128)(2,1)S(1)}, u32[]{:S(2)}, u32[]{:S(2)}) collective-permute-start(bf16[2064,128]{1,0:T(8,128)(2,1)S(1)} %collective-permute-done.9.refs_4_), channel_id=1, source_target_pairs={{0,4},{4,0},{8,12},{12,8},{16,20},{20,16},{24,28},{28,24},{32,36},... | collective-permute-start | bytes 1585160 | tf_op jit(solution)/shard_map/ppermute | solution.py:69
  79.9 21.1 %collective-permute-start.13 = (bf16[2,128,512]{2,1,0:T(8,128)(2,1)S(1)}, bf16[2,128,512]{2,1,0:T(8,128)(2,1)S(1)}, u32[]{:S(2)}, u32[]{:S(2)}) collective-permute-start(bf16[2,128,512]{2,1,0:T(8,128)(2,1)S(1)} %get-tuple-element.68), channel_id=1, source_target_pairs={{0,32},{4,36},{8,40},{12,44},{16,48},{20,52},{24,56},{28,60},{32,6... | collective-permute-start | bytes 786440 | tf_op jit(solution)/shard_map/ppermute | solution.py:69
  80.9 20.1 %collective-permute-start.14 = (bf16[2,128,512]{2,1,0:T(8,128)(2,1)S(1)}, bf16[2,128,512]{2,1,0:T(8,128)(2,1)S(1)}, u32[]{:S(2)}, u32[]{:S(2)}) collective-permute-start(bf16[2,128,512]{2,1,0:T(8,128)(2,1)S(1)} %get-tuple-element.69), channel_id=1, source_target_pairs={{0,96},{4,100},{8,104},{12,108},{16,112},{20,116},{24,120},{28,124... | collective-permute-start | bytes 786440 | tf_op jit(solution)/shard_map/ppermute | solution.py:69
  82.6 18.4 %collective-permute-start.15 = (bf16[2,128,512]{2,1,0:T(8,128)(2,1)S(1)}, bf16[2,128,512]{2,1,0:T(8,128)(2,1)S(1)}, u32[]{:S(2)}, u32[]{:S(2)}) collective-permute-start(bf16[2,128,512]{2,1,0:T(8,128)(2,1)S(1)} %get-tuple-element.70), channel_id=1, source_target_pairs={{0,64},{4,68},{8,72},{12,76},{16,80},{20,84},{24,88},{28,92},{32,9... | collective-permute-start | bytes 786440 | tf_op jit(solution)/shard_map/ppermute | solution.py:69
  101.0 8.4 %collective-permute-start.17 = (bf16[2,128,512]{2,1,0:T(8,128)(2,1)S(1)}, bf16[2,128,512]{2,1,0:T(8,128)(2,1)S(1)}, u32[]{:S(2)}, u32[]{:S(2)}) collective-permute-start(bf16[2,128,512]{2,1,0:T(8,128)(2,1)S(1)} %get-tuple-element.87), channel_id=1, source_target_pairs={{0,32},{4,36},{8,40},{12,44},{16,48},{20,52},{24,56},{28,60},{32,6... | collective-permute-start | bytes 786440 | tf_op jit(solution)/shard_map/ppermute | solution.py:69
  101.4 8.0 %collective-permute-start.18 = (bf16[2,128,512]{2,1,0:T(8,128)(2,1)S(1)}, bf16[2,128,512]{2,1,0:T(8,128)(2,1)S(1)}, u32[]{:S(2)}, u32[]{:S(2)}) collective-permute-start(bf16[2,128,512]{2,1,0:T(8,128)(2,1)S(1)} %get-tuple-element.88), channel_id=1, source_target_pairs={{0,96},{4,100},{8,104},{12,108},{16,112},{20,116},{24,120},{28,124... | collective-permute-start | bytes 786440 | tf_op jit(solution)/shard_map/ppermute | solution.py:69
  103.8 10.7 %collective-permute-start.19 = (bf16[2,128,512]{2,1,0:T(8,128)(2,1)S(1)}, bf16[2,128,512]{2,1,0:T(8,128)(2,1)S(1)}, u32[]{:S(2)}, u32[]{:S(2)}) collective-permute-start(bf16[2,128,512]{2,1,0:T(8,128)(2,1)S(1)} %get-tuple-element.89), channel_id=1, source_target_pairs={{0,64},{4,68},{8,72},{12,76},{16,80},{20,84},{24,88},{28,92},{32,9... | collective-permute-start | bytes 786440 | tf_op jit(solution)/shard_map/ppermute | solution.py:69
  105.5 11.9 %collective-permute-start.16 = (f32[2,64,512]{2,1,0:T(8,128)S(1)}, f32[2,64,512]{2,1,0:T(8,128)S(1)}, u32[]{:S(2)}, u32[]{:S(2)}) collective-permute-start(f32[2,64,512]{2,1,0:T(8,128)S(1)} %get-tuple-element.92), channel_id=1, source_target_pairs={{0,4},{4,0},{8,12},{12,8},{16,20},{20,16},{24,28},{28,24},{32,36},... | collective-permute-start | bytes 786440 | tf_op jit(solution)/shard_map/ppermute | solution.py:69
  115.2 3.4 %collective-permute-start.20 = (f32[2,64,512]{2,1,0:T(8,128)S(1)}, f32[2,64,512]{2,1,0:T(8,128)S(1)}, u32[]{:S(2)}, u32[]{:S(2)}) collective-permute-start(f32[2,64,512]{2,1,0:T(8,128)S(1)} %get-tuple-element.94), channel_id=1, source_target_pairs={{0,4},{4,0},{8,12},{12,8},{16,20},{20,16},{24,28},{28,24},{32,36},... | collective-permute-start | bytes 786440 | tf_op jit(solution)/shard_map/ppermute | solution.py:69
